TPU v7x, 128 devices: a whole 4x4x4 slice. The times are simulated.
128 devices in a mesh: island: 8 (over z_lo, y), fsdp: 16 (over z_hi, x, core).
Axes of the slice: x: 4, y: 4, z: 4 (z_hi: 2, z_lo: 2; z = z_hi * 2 + z_lo), core: 2. Of those that a mesh axis runs over, the one named last changes fastest.
Arguments:
- weights: bfloat16 [4096, 14336], P(None, 'fsdp'), may hold values from -3 to 3
- momentum: bfloat16 [4096, 14336], P(None, 'fsdp'), may hold values from -0.59765625 to 0.59765625
- table: bfloat16 [2048, 4096], P(None, 'fsdp'), may hold values from -6 to 6
- token_ids: int32 [8, 2, 896], P('island'), may hold values from 0 to 2047
- cotangent: bfloat16 [8, 2, 896, 14336], P('island', None, None, 'fsdp'), may hold values from -6 to 6
Outputs:
- new_weights: bfloat16 [4096, 14336], P(None, 'fsdp')
All inputs are finite; a program needn't handle non-finite values.
Results may differ from a plain program's by a relative error of at most 0.005.
Values may be sent and summed in bfloat16 or wider, within the bound.
No kernel may reach another device: no remote copies, remote signals or barrier semaphores. Data moves between devices by JAX's collectives and lax.ppermute only.
A program may use at most 128 MiB of HBM per device.

v0:
```python
import math

import jax
import jax.numpy as jnp
from jax import lax
from jax.sharding import PartitionSpec as P

beta_one = 0.9
beta_two = 0.95
adam_eps = 0.0001
inner_rate = 0.1
decay_rate = 0.1
outer_rate = 0.7
outer_moment = 0.9


def silu_slope(hidden):
    sigma = jax.nn.sigmoid(hidden)
    return sigma * (1.0 + hidden * (1.0 - sigma))


def grad_rows(inputs, upstream):
    return lax.dot_general(
        inputs, upstream, (((0,), (0,)), ((), ())), preferred_element_type=jnp.float32
    )


def make_upstream(hidden, island_cot):
    return (island_cot.astype(jnp.float32) * silu_slope(hidden) / island_cot.shape[0]).astype(
        jnp.bfloat16
    )


def inner_grad(x_local, work, island_cot, scale):
    whole = lax.all_gather(x_local, "fsdp", axis=1, tiled=True)
    hidden = jnp.dot(whole, work, preferred_element_type=jnp.float32) * scale
    upstream = make_upstream(hidden, island_cot)
    return grad_rows(whole, upstream) * scale


def outer_update(base, prior, mean):
    moment = outer_moment * prior.astype(jnp.float32) + mean
    return (base - outer_rate * (mean + outer_moment * moment)).astype(jnp.bfloat16)


def body(weights, momentum, table, token_ids, cotangent):
    scale = 1.0 / math.sqrt(weights.shape[0])
    start = weights.astype(jnp.float32)
    local = start
    first = jnp.zeros(start.shape, jnp.float32)
    second = jnp.zeros(start.shape, jnp.float32)
    for step in range(token_ids.shape[1]):
        work = weights if step == 0 else local.astype(jnp.bfloat16)
        x_local = jnp.take(table, token_ids[0, step], axis=0)
        grad = inner_grad(x_local, work, cotangent[0, step], scale)
        first = beta_one * first + (1.0 - beta_one) * grad
        second = beta_two * second + (1.0 - beta_two) * grad * grad
        m_hat = first / (1.0 - beta_one ** (step + 1))
        v_hat = second / (1.0 - beta_two ** (step + 1))
        local = local - inner_rate * (m_hat / (jnp.sqrt(v_hat) + adam_eps) + decay_rate * local)
    delta = (start - local).astype(jnp.bfloat16).astype(jnp.float32)
    islands = lax.axis_size("island")
    total = lax.psum(delta.astype(jnp.bfloat16), "island").astype(jnp.float32)
    return outer_update(start, momentum, total / islands)


def solution(mesh):
    placed = (
        P(None, "fsdp"),
        P(None, "fsdp"),
        P(None, "fsdp"),
        P("island", None, None),
        P("island", None, None, "fsdp"),
    )
    return jax.shard_map(
        body, mesh=mesh, in_specs=placed, out_specs=P(None, "fsdp"), check_vma=False
    )
```

profile of v0, /device:TPU:70, one launch (start us, length us, event | category | flops | bytes accessed | tf_op | source)
XLA Modules:
  0.0 402.0 jit_solution(5329779110135888894)
XLA Ops:
  6.5 0.0 copy-start
  6.5 0.0 all-gather.3.cloned.1.call-start
  6.5 0.8 slice_reduce_fusion.1
  7.4 0.4 copy-done
  7.8 3.5 gather_fusion
  11.3 1.0 broadcast_select_fusion.1
  12.2 0.0 all-gather.3.cloned.1.call-update
  12.3 0.0 all-gather.5.cloned.1.call-start
  12.3 3.5 gather_fusion.1
  15.8 1.0 broadcast_select_fusion
  16.8 0.0 all-gather.5.cloned.1.call-update
  16.9 0.0 all-reduce.2.cloned.1.call-start
  16.9 68.6 %all-gather.3.cloned.1.call-done = bf16[896,4096]{1,0:T(8,128)(2,1)} async-done(((bf16[896,256]{1,0:T(8,128)(2,1)}), bf16[896,4096]{1,0:T(8,128)(2,1)}) %all-gather.3.cloned.1.call-update) | async-done | bytes 7340048 | tf_op jit(solution)/shard_map/all_gather | solution.py:35
  85.5 28.5 %fusion.10 = f32[4096,896]{1,0:T(8,128)} fusion(bf16[896,4096]{1,0:T(8,128)(2,1)} %all-gather.3.cloned.1.call-done, bf16[4096,896]{1,0:T(8,128)(2,1)} %param.7, bf16[1,2,896,896]{3,2,1,0:T(8,128)(2,1)} %param.11), kind=kOutput, calls=%fused_computation.19 | convolution fusion | flops 13162971136 | bytes 38305792 | tf_op jit(solution)/shard_map/dot_general | solution.py:23
  114.0 46.9 %all-gather.5.cloned.1.call-done = bf16[896,4096]{1,0:T(8,128)(2,1)} async-done(((bf16[896,256]{1,0:T(8,128)(2,1)}), bf16[896,4096]{1,0:T(8,128)(2,1)}) %all-gather.5.cloned.1.call-update) | async-done | bytes 7340048 | tf_op jit(solution)/shard_map/all_gather | solution.py:35
  160.9 0.0 copy-start.2
  160.9 22.1 %fusion.7.clone.4 = bf16[896,896]{1,0:T(8,128)(2,1)} fusion(bf16[896,4096]{1,0:T(8,128)(2,1)} %all-gather.5.cloned.1.call-done, f32[4096,896]{1,0:T(8,128)} %fusion.10, bf16[4096,896]{1,0:T(8,128)(2,1)} %param.7, bf16[1,2,896,896]{3,2,1,0:T(8,128)(2,1)} %param.11), kind=kOutput, calls=%fused_computation.15.clone.clone.clone.1 | convolution fusion | flops 6630342656 | bytes 32571392 | tf_op jit(solution)/shard_map/dot_general | solution.py:36
  183.0 0.0 copy-done.2
  183.0 34.2 %fusion.2 = bf16[4096,896]{1,0:T(8,128)(2,1)} fusion(bf16[4096,896]{1,0:T(8,128)(2,1)} %param.7, f32[4096,896]{1,0:T(8,128)} %fusion.10, bf16[896,4096]{1,0:T(8,128)(2,1)S(1)} %copy-done.2, bf16[896,896]{1,0:T(8,128)(2,1)} %fusion.7.clone.4), kind=kOutput, calls=%fused_computation.8 | convolution fusion | flops 6683099136 | bytes 38305792 | tf_op jit(solution)/shard_map/dot_general | solution.py:23
  217.2 0.0 all-reduce.2.cloned.1.call-update
  217.2 166.2 %all-reduce.2.cloned.1.call-done = bf16[4096,896]{1,0:T(8,128)(2,1)} async-done(((bf16[4096,896]{1,0:T(8,128)(2,1)}), bf16[4096,896]{1,0:T(8,128)(2,1)}) %all-reduce.2.cloned.1.call-update) | async-done | bytes 7340048 | tf_op jit(solution)/shard_map/psum | solution.py:63
  383.4 0.0 copy-start.1
  383.4 12.1 %fusion.3 = bf16[4096,896]{1,0:T(8,128)(2,1)} fusion(bf16[4096,896]{1,0:T(8,128)(2,1)} %param.7, bf16[4096,896]{1,0:T(8,128)(2,1)} %param.8, bf16[4096,896]{1,0:T(8,128)(2,1)} %all-reduce.2.cloned.1.call-done), kind=kLoop, calls=%fused_computation.9 | loop fusion | flops 40370176 | bytes 29360128 | tf_op jit(solution)/shard_map/convert_element_type | solution.py:43
  395.4 0.0 copy-done.1
  (6 shorter events, 0.0 us)
Async XLA Ops:
  6.5 1.3 copy-start
  6.5 78.9 %all-gather.3.cloned.1.call-start = ((), (), s32[]{:S(2)}) async-start(), calls=%async_computation | async-start | bytes 7798784 | tf_op jit(solution)/shard_map/all_gather | solution.py:35
  12.3 148.7 %all-gather.5.cloned.1.call-start = ((), (), s32[]{:S(2)}) async-start(), calls=%async_computation.1 | async-start | bytes 7798784 | tf_op jit(solution)/shard_map/all_gather | solution.py:35
  16.9 366.5 %all-reduce.2.cloned.1.call-start = ((), (), s32[]{:S(2)}) async-start(), calls=%async_computation.2 | async-start | bytes 14680064 | tf_op jit(solution)/shard_map/psum | solution.py:63
  160.9 22.1 %copy-start.2 = (bf16[896,4096]{1,0:T(8,128)(2,1)S(1)}, bf16[896,4096]{1,0:T(8,128)(2,1)}, u32[]{:S(2)}) copy-start(bf16[896,4096]{1,0:T(8,128)(2,1)} %all-gather.5.cloned.1.call-done) | copy-start | bytes 22020100
  383.4 12.1 %copy-start.1 = (bf16[2048,256]{1,0:T(8,128)(2,1)S(1)}, bf16[2048,256]{1,0:T(8,128)(2,1)}, u32[]{:S(2)}) copy-start(bf16[2048,256]{1,0:T(8,128)(2,1)} %param.9) | copy-start | bytes 3145732
Sparse Core Ops, SparseCore 0:
  12.4 73.0 all-gather.2
  87.7 73.1 all-gather.4
  217.3 166.0 all-reduce.1
where the time goes:
time: 404 us; the launch traced here: 402 us
  waiting for transfers between devices  282 us (70%)
  matrix products  84.8 us (21%)
  other arithmetic  14 us (3%)
  between operations  13.2 us (3%)
  local copies, waits for them, and re-layouts  8.19 us (2%)
    psum x1, waiting for transfers between devices, body(): total = lax.psum(delta.astype(jnp.bfloat16), 'island').astype(jnp.float32)  166 us
    all_gather x2, waiting for transfers between devices, inner_grad(): whole = lax.all_gather(x_local, 'fsdp', axis=1, tiled=True)  115 us
    dot_general x2, matrix products, grad_rows(): lax.dot_general(inputs, upstream, (((0,), (0,)), ((), ())), preferred_ele...  62.7 us
    dot_general x1, matrix products, inner_grad(): hidden = jnp.dot(whole, work, preferred_element_type=jnp.float32) * scale  22.1 us
    convert_element_type x1, other arithmetic, outer_update(): (base - outer_rate * (mean + outer_moment * moment)).astype(jnp.bfloat16)  12.1 us
  transfers between devices with their start and end apart: 3, of which 3 were waited for; matrix products, arithmetic and copies ran while one was open for 8% of the time, Pallas kernels for 0%

commit v1 on v0

v1 whole, which is shorter than its diff:
```python
import math

import jax
import jax.numpy as jnp
from jax import lax
from jax.experimental import pallas as pl
from jax.experimental.pallas import tpu as pltpu
from jax.sharding import PartitionSpec as P

beta_one = 0.9
beta_two = 0.95
adam_eps = 0.0001
inner_rate = 0.1
decay_rate = 0.1
outer_rate = 0.7
outer_moment = 0.9

MB = 1 << 20
AXES = ("island", "fsdp")
XA, XB = 1, 3
SPLIT = (64, 48)
ROWS_Y = 768
PARTS = ((0, 1408), (1408, 1408), (2816, 1280))
ORDERS = ((1, 3, 4), (3, 4, 1), (4, 1, 3))


def swap(a, partner):
    pairs = []
    for zlo in range(2):
        for y in range(4):
            for zhi in range(2):
                for x in range(4):
                    for c in range(2):
                        px, py, pz, pc = partner(x, y, zhi * 2 + zlo, c)
                        me = (zlo * 4 + y) * 16 + zhi * 8 + x * 2 + c
                        to = ((pz % 2) * 4 + py) * 16 + (pz // 2) * 8 + px * 2 + pc
                        pairs.append((me, to))
    return lax.ppermute(a, AXES, pairs)


def over_x(a, first):
    return swap(a, lambda x, y, z, c: (x ^ (XA if (c == 0) == first else XB), y, z, c))


def over_y(a, first):
    return swap(a, lambda x, y, z, c: (x, y ^ (XA if (c == 0) == first else XB), z, c))


def over_z(a):
    return swap(a, lambda x, y, z, c: (x, y, z ^ 3, c))


def over_core(a):
    return swap(a, lambda x, y, z, c: (x, y, z, c ^ 1))


def over_island(a, mask):
    return swap(a, lambda x, y, z, c: (x, y ^ (mask & 3), z ^ (mask >> 2), c))


def slope(hidden):
    sigma = 0.5 * (1.0 + jnp.tanh(0.5 * hidden))
    return sigma * (1.0 + hidden * (1.0 - sigma))


def gather_table(table, island, fsdp):
    rows, width = table.shape
    x, core, zhi, y = (fsdp // 2) % 4, fsdp % 2, fsdp // 8, island % 4
    span = ROWS_Y // 4
    part_y = lax.dynamic_slice(table, (y * span, 0), (span, width))
    part_x = table[ROWS_Y:]
    y0 = jnp.concatenate([part_y, over_z(part_y)])
    x_z = over_z(part_x)
    y1 = over_x(y0, True)
    y2 = over_x(jnp.concatenate([y0, y1]), False)
    x1 = over_x(part_x, True)
    x1z = over_x(x_z, True)
    x2 = over_x(jnp.concatenate([part_x, x1]), False)
    x2z = over_x(jnp.concatenate([x_z, x1z]), False)
    all8 = jnp.concatenate([y0, y1, y2])
    w1 = over_y(all8, True)
    w2 = over_y(jnp.concatenate([all8, w1]), False)
    own = [table, x_z, x1, x1z, x2, x2z, all8, w1, w2]
    other = [over_core(a) for a in own]

    copies, offsets = [], []

    def place(piece, source, count, row, xx, zz, cc):
        copies.append((piece, source, count))
        offsets.append((row, 256 * (zz * 8 + xx * 2 + cc)))

    for q in range(2):
        cc = core ^ q
        d1 = jnp.where(cc == 0, XA, XB)
        d2 = XA + XB - d1
        base = 9 * q
        n = rows - ROWS_Y
        place(base, 0, rows, 0, x, zhi, cc)
        place(base + 1, 0, n, ROWS_Y, x, zhi ^ 1, cc)
        place(base + 2, 0, n, ROWS_Y, x ^ d1, zhi, cc)
        place(base + 3, 0, n, ROWS_Y, x ^ d1, zhi ^ 1, cc)
        place(base + 4, 0, n, ROWS_Y, x ^ d2, zhi, cc)
        place(base + 4, n, n, ROWS_Y, x ^ 2, zhi, cc)
        place(base + 5, 0, n, ROWS_Y, x ^ d2, zhi ^ 1, cc)
        place(base + 5, n, n, ROWS_Y, x ^ 2, zhi ^ 1, cc)
        xs = [x, x ^ d1, x ^ d2, x ^ 2]
        for piece, start, yy in (
            (base + 6, 0, y),
            (base + 7, 0, y ^ d1),
            (base + 8, 0, y ^ d2),
            (base + 8, 8 * span, y ^ 2),
        ):
            for block in range(1, 8):
                place(piece, start + block * span, span, yy * span, xs[block // 2], zhi ^ (block % 2), cc)
    where = jnp.stack([jnp.stack([jnp.asarray(v, jnp.int32) for v in pair]) for pair in offsets])

    def kernel(where_ref, *refs):
        pieces, whole, sems = refs[:18], refs[18], refs[19]
        started = []
        for i, (piece, source, count) in enumerate(copies):
            row = pl.multiple_of(where_ref[i, 0], 16)
            col = pl.multiple_of(where_ref[i, 1], 256)
            copy = pltpu.make_async_copy(
                pieces[piece].at[pl.ds(source, count), :],
                whole.at[pl.ds(row, count), pl.ds(col, 256)],
                sems.at[i],
            )
            copy.start()
            started.append(copy)
        for copy in started:
            copy.wait()

    full = width * 16
    return pl.pallas_call(
        kernel,
        in_specs=[pl.BlockSpec(memory_space=pltpu.SMEM)] + [pl.BlockSpec(memory_space=pl.ANY)] * 18,
        out_specs=pl.BlockSpec(memory_space=pltpu.VMEM),
        out_shape=pltpu.VMEM((rows, full), table.dtype),
        scratch_shapes=[pltpu.SemaphoreType.DMA((len(copies),))],
        compiler_params=pltpu.CompilerParams(vmem_limit_bytes=20 * MB),
        cost_estimate=pl.CostEstimate(flops=0, bytes_accessed=2 * rows * full * 2, transcendentals=0),
        name="gather_table",
    )(where, *own, *other)


def add_by_row(cot, ids, rows):
    count, units, tokens = cot.shape

    def kernel(cot_ref, ids_ref, *outs):
        tile = 512
        for t in range(rows // tile):
            row = lax.broadcasted_iota(jnp.int32, (tile, tokens), 0) + t * tile
            hot = jnp.where(row == ids_ref[0], 1.0, 0.0).astype(jnp.bfloat16)
            total = lax.dot_general(
                cot_ref[0], hot, (((1,), (1,)), ((), ())), preferred_element_type=jnp.float32
            ).astype(jnp.bfloat16)
            at = 0
            for out, size in zip(outs, SPLIT):
                out[0, :, t * tile : (t + 1) * tile] = total[at : at + size]
                at += size

    return pl.pallas_call(
        kernel,
        grid=(count,),
        in_specs=[
            pl.BlockSpec((1, units, tokens), lambda i: (i, 0, 0)),
            pl.BlockSpec((1, 1, tokens), lambda i: (i, 0, 0)),
        ],
        out_specs=[pl.BlockSpec((1, size, rows), lambda i: (i, 0, 0)) for size in SPLIT],
        out_shape=[jax.ShapeDtypeStruct((count, size, rows), jnp.bfloat16) for size in SPLIT],
        compiler_params=pltpu.CompilerParams(vmem_limit_bytes=24 * MB),
        cost_estimate=pl.CostEstimate(
            flops=2 * count * units * tokens * rows, bytes_accessed=count * units * (tokens + rows) * 2, transcendentals=0
        ),
        name="add_by_row",
    )(cot, ids)


def first_step(table, w, cots, tokens):
    rows, width = table.shape
    units = w.shape[0]
    scale = 1.0 / math.sqrt(width)
    block = 512

    def kernel(table_ref, w_ref, cot_ref, wb_ref, work_ref, grad_ref, up_ref):
        i = pl.program_id(0)

        @pl.when(i == 0)
        def _():
            for t in range(rows // block):
                at = slice(t * block, (t + 1) * block)
                hidden = lax.dot_general(
                    w_ref[...], table_ref[at, :], (((1,), (1,)), ((), ())), preferred_element_type=jnp.float32
                )
                factor = slope(hidden * scale) * (1.0 / tokens)
                for m in range(8):
                    up_ref[m * units : (m + 1) * units, at] = (cot_ref[m, :, at].astype(jnp.float32) * factor).astype(
                        jnp.bfloat16
                    )

        cols = pl.ds(pl.multiple_of(i * block, block), block)
        grad = jnp.dot(up_ref[...], table_ref[:, cols], preferred_element_type=jnp.float32) * scale
        grad_ref[...] = grad.astype(jnp.bfloat16)
        base = wb_ref[...].astype(jnp.float32)
        for m in range(8):
            g = grad[m * units : (m + 1) * units]
            local = base - inner_rate * (g / (jnp.abs(g) + adam_eps) + decay_rate * base)
            work_ref[m * units : (m + 1) * units, :] = local.astype(jnp.bfloat16)

    return pl.pallas_call(
        kernel,
        grid=(width // block,),
        in_specs=[
            pl.BlockSpec(memory_space=pltpu.VMEM),
            pl.BlockSpec((units, width), lambda i: (0, 0)),
            pl.BlockSpec((8, units, rows), lambda i: (0, 0, 0)),
            pl.BlockSpec((units, block), lambda i: (0, i)),
        ],
        out_specs=[pl.BlockSpec((8 * units, block), lambda i: (0, i))] * 2,
        out_shape=[jax.ShapeDtypeStruct((8 * units, width), jnp.bfloat16)] * 2,
        scratch_shapes=[pltpu.VMEM((8 * units, rows), jnp.bfloat16)],
        compiler_params=pltpu.CompilerParams(vmem_limit_bytes=36 * MB),
        cost_estimate=pl.CostEstimate(
            flops=18 * units * rows * width, bytes_accessed=rows * width * 2 + 36 * units * width, transcendentals=0
        ),
        name="first_step",
    )(table, w, cots, w)


def second_upstream(table, work, cots, tokens):
    rows, width = table.shape
    many = work.shape[0]
    scale = 1.0 / math.sqrt(width)
    block = 512

    def kernel(table_ref, work_ref, cot_ref, up_ref):
        at = pl.ds(pl.multiple_of(pl.program_id(0) * block, block), block)
        hidden = lax.dot_general(
            work_ref[...], table_ref[at, :], (((1,), (1,)), ((), ())), preferred_element_type=jnp.float32
        )
        up_ref[...] = (cot_ref[...].astype(jnp.float32) * (slope(hidden * scale) * (1.0 / tokens))).astype(jnp.bfloat16)

    return pl.pallas_call(
        kernel,
        grid=(rows // block,),
        in_specs=[
            pl.BlockSpec(memory_space=pltpu.VMEM),
            pl.BlockSpec((many, width), lambda i: (0, 0)),
            pl.BlockSpec((many, block), lambda i: (0, i)),
        ],
        out_specs=pl.BlockSpec((many, block), lambda i: (0, i)),
        out_shape=jax.ShapeDtypeStruct((many, rows), jnp.bfloat16),
        compiler_params=pltpu.CompilerParams(vmem_limit_bytes=36 * MB),
        cost_estimate=pl.CostEstimate(
            flops=2 * many * rows * width, bytes_accessed=rows * width * 2 + 2 * many * width, transcendentals=0
        ),
        name="second_upstream",
    )(table, work, cots.reshape(many, rows))


def outer_step(table, up, grads, w, momentum):
    rows, width = table.shape
    units = w.shape[0]
    scale = 1.0 / math.sqrt(width)
    block = 512

    def kernel(table_ref, up_ref, grad_ref, w_ref, mom_ref, out_ref):
        cols = pl.ds(pl.multiple_of(pl.program_id(0) * block, block), block)
        second_grad = jnp.dot(up_ref[...], table_ref[:, cols], preferred_element_type=jnp.float32) * scale
        start = w_ref[...].astype(jnp.float32)
        total = jnp.zeros(start.shape, jnp.float32)
        for m in range(8):
            span = slice(m * units, (m + 1) * units)
            g0 = grad_ref[span, :].astype(jnp.float32)
            g1 = second_grad[span]
            local = start - inner_rate * (g0 / (jnp.abs(g0) + adam_eps) + decay_rate * start)
            first = beta_one * (1.0 - beta_one) * g0 + (1.0 - beta_one) * g1
            second = beta_two * (1.0 - beta_two) * g0 * g0 + (1.0 - beta_two) * g1 * g1
            m_hat = first * (1.0 / (1.0 - beta_one**2))
            v_hat = second * (1.0 / (1.0 - beta_two**2))
            local = local - inner_rate * (m_hat / (jnp.sqrt(v_hat) + adam_eps) + decay_rate * local)
            total = total + (start - local).astype(jnp.bfloat16).astype(jnp.float32)
        mean = total * (1.0 / 8.0)
        moment = outer_moment * mom_ref[...].astype(jnp.float32) + mean
        out_ref[...] = (start - outer_rate * (mean + outer_moment * moment)).astype(jnp.bfloat16)

    return pl.pallas_call(
        kernel,
        grid=(width // block,),
        in_specs=[
            pl.BlockSpec(memory_space=pltpu.VMEM),
            pl.BlockSpec((8 * units, rows), lambda i: (0, 0)),
            pl.BlockSpec((8 * units, block), lambda i: (0, i)),
            pl.BlockSpec((units, block), lambda i: (0, i)),
            pl.BlockSpec((units, block), lambda i: (0, i)),
        ],
        out_specs=pl.BlockSpec((units, block), lambda i: (0, i)),
        out_shape=jax.ShapeDtypeStruct((units, width), jnp.bfloat16),
        compiler_params=pltpu.CompilerParams(vmem_limit_bytes=36 * MB),
        cost_estimate=pl.CostEstimate(
            flops=16 * units * rows * width, bytes_accessed=rows * width * 2 + 36 * units * width, transcendentals=0
        ),
        name="outer_step",
    )(table, up, grads, w, momentum)


def spread(new):
    found = []
    for (low, size), (e1, e2, e3) in zip(PARTS, ORDERS):
        own = new[:, low : low + size]
        r1 = over_island(own, e1)
        two = jnp.concatenate([own, r1])
        r2 = over_island(two, e2)
        r3 = over_island(jnp.concatenate([two, r2]), e3)
        found.append([(own, (0,)), (r1, (e1,)), (r2, (e2, e2 ^ e1)), (r3, (e3, e3 ^ e1, e3 ^ e2, e3 ^ e2 ^ e1))])
    return found


def assemble(chunks, island, units, width):
    operands, copies, masks = [], [[] for _ in PARTS], []
    at = 0
    for size, found in zip(SPLIT, chunks):
        for p, pieces in enumerate(found):
            for array, froms in pieces:
                for j, mask in enumerate(froms):
                    copies[p].append((len(operands), j * size, size, at, mask))
                operands.append(array)
        at += size
    total = sum(len(c) for c in copies)
    n = len(operands)
    where = jnp.stack([(island ^ m) * units for m in range(8)]).astype(jnp.int32)

    def kernel(where_ref, *refs):
        arrays, out, held, turned, sems, out_sems = refs[:n], refs[n], refs[n + 1], refs[n + 2], refs[n + 3], refs[n + 4]
        k, waits = 0, []
        for (low, length), group in zip(PARTS, copies):
            mine = []
            for piece, source, size, place, mask in group:
                row = pl.multiple_of(where_ref[mask] + place, 16)
                copy = pltpu.make_async_copy(
                    arrays[piece].at[pl.ds(source, size), :],
                    held.at[pl.ds(row, size), pl.ds(low, length)],
                    sems.at[k],
                )
                copy.start()
                mine.append(copy)
                k += 1
            waits.append(mine)
        outs = []
        for p, ((low, length), mine) in enumerate(zip(PARTS, waits)):
            for copy in mine:
                copy.wait()
            for col in range(low, low + length, 128):
                turned[col : col + 128, :] = held[:, col : col + 128].T
            copy = pltpu.make_async_copy(
                turned.at[pl.ds(low, length), :], out.at[pl.ds(low, length), :], out_sems.at[p]
            )
            copy.start()
            outs.append(copy)
        for copy in outs:
            copy.wait()

    return pl.pallas_call(
        kernel,
        in_specs=[pl.BlockSpec(memory_space=pltpu.SMEM)] + [pl.BlockSpec(memory_space=pl.ANY)] * n,
        out_specs=pl.BlockSpec(memory_space=pl.ANY),
        out_shape=jax.ShapeDtypeStruct((width, 8 * units), jnp.bfloat16),
        scratch_shapes=[
            pltpu.VMEM((8 * units, width), jnp.bfloat16),
            pltpu.VMEM((width, 8 * units), jnp.bfloat16),
            pltpu.SemaphoreType.DMA((total,)),
            pltpu.SemaphoreType.DMA((len(PARTS),)),
        ],
        compiler_params=pltpu.CompilerParams(vmem_limit_bytes=24 * MB),
        cost_estimate=pl.CostEstimate(flops=0, bytes_accessed=32 * units * width, transcendentals=0),
        name="assemble",
    )(where, *operands)


def body(weights, momentum, table, token_ids, cotangent):
    island, fsdp = lax.axis_index("island"), lax.axis_index("fsdp")
    width, hidden_units = weights.shape
    steps, tokens = token_ids.shape[1:]
    rows = table.shape[0]
    units = hidden_units // 8

    turned = jnp.swapaxes(cotangent[0], 1, 2)
    every_id = lax.all_gather(token_ids[0], "island", axis=0)
    sums = []
    for step in range(steps):
        blocks = [
            lax.dynamic_slice(turned[step], ((island ^ m) * units, 0), (units, tokens)) for m in range(8)
        ]
        arrived = jnp.stack([blocks[0]] + [over_island(blocks[m], m) for m in range(1, 8)])
        ids = jnp.stack([lax.dynamic_index_in_dim(every_id[:, step], island ^ m, 0) for m in range(8)])
        sums.append(add_by_row(arrived, ids, rows))

    def mine(a):
        return lax.dynamic_slice(a.T, (island * units, 0), (units, width))

    w, mom = mine(weights), mine(momentum)
    whole = gather_table(table, island, fsdp)
    chunks, at = [], 0
    for c, size in enumerate(SPLIT):
        w_c, mom_c = w[at : at + size], mom[at : at + size]
        work, grads = first_step(whole, w_c, sums[0][c], tokens)
        up = second_upstream(whole, work, sums[1][c], tokens)
        chunks.append(spread(outer_step(whole, up, grads, w_c, mom_c)))
        at += size
    return assemble(chunks, island, units, width)


def solution(mesh):
    placed = (
        P(None, "fsdp"),
        P(None, "fsdp"),
        P(None, "fsdp"),
        P("island", None, None),
        P("island", None, None, "fsdp"),
    )
    return jax.shard_map(body, mesh=mesh, in_specs=placed, out_specs=P(None, "fsdp"), check_vma=False)
```

time: 404 us -> 429 us (1.062)
  waiting for transfers between devices: 282 us -> 105 us
  Pallas kernels: 0 us -> 164 us
  matrix products: 84.8 us -> 0 us
  starting transfers between devices: 0.09 us -> 59 us
  local copies, waits for them, and re-layouts: 8.19 us -> 52.8 us
  blocking collectives: 0 us -> 28.3 us
  between operations: 13.2 us -> 1.33 us
    psum x1 -> x0, waiting for transfers between devices: 166 us -> none  [body(): total = lax.psum(delta.astype(jnp.bfloat16), 'island').astype(jnp.float32)]
    pallas_call x0 -> x10, Pallas kernels: none -> 164 us  [the longest x2 56.6 us: outer_step(): pl.pallas_call(kernel, grid=(width // block,), in_specs=[pl.BlockSpec(mem...]
    all_gather x2 -> x0, waiting for transfers between devices: 115 us -> none  [inner_grad(): whole = lax.all_gather(x_local, 'fsdp', axis=1, tiled=True)]
    ppermute x0 -> x51, waiting for transfers between devices: none -> 105 us  [swap(): return lax.ppermute(a, AXES, pairs)]
    dot_general x3 -> x0, matrix products: 84.8 us -> none  [the longest x2 62.7 us: grad_rows(): lax.dot_general(inputs, upstream, (((0,), (0,)), ((), ())), preferred_ele...]
    ppermute x0 -> x51, starting transfers between devices: none -> 59 us  [swap(): return lax.ppermute(a, AXES, pairs)]
    all_gather x0 -> x1, blocking collectives: none -> 28.3 us  [body(): every_id = lax.all_gather(token_ids[0], 'island', axis=0)]
    unnamed x6 -> x126, local copies, waits for them, and re-layouts: 0.4 us -> 27.8 us
  transfers between devices with their start and end apart: 3 -> 51, of which waited for: 3 -> 21; matrix products, arithmetic and copies ran while one was open for 8% -> 12% of each run, Pallas kernels for 0% -> 5%
where the time goes in v1:
time: 429 us; the launch traced here: 424 us
  Pallas kernels  164 us (38%)
  waiting for transfers between devices  105 us (24%)
  starting transfers between devices  59 us (14%)
  local copies, waits for them, and re-layouts  52.8 us (12%)
  blocking collectives  28.3 us (7%)
  other arithmetic  13.2 us (3%)
    ppermute x51, waiting for transfers between devices, swap(): return lax.ppermute(a, AXES, pairs)  105 us
    ppermute x51, starting transfers between devices, swap(): return lax.ppermute(a, AXES, pairs)  59 us
    pallas_call x2, Pallas kernels, outer_step(): pl.pallas_call(kernel, grid=(width // block,), in_specs=[pl.BlockSpec(mem...  56.6 us
    pallas_call x2, Pallas kernels, first_step(): pl.pallas_call(kernel, grid=(width // block,), in_specs=[pl.BlockSpec(mem...  45.7 us
    pallas_call x2, Pallas kernels, second_upstream(): pl.pallas_call(kernel, grid=(rows // block,), in_specs=[pl.BlockSpec(memo...  31.2 us
    all_gather x1, blocking collectives, body(): every_id = lax.all_gather(token_ids[0], 'island', axis=0)  28.3 us
    unnamed x126, local copies, waits for them, and re-layouts  27.8 us
    pallas_call x2, Pallas kernels, add_by_row(): pl.pallas_call(kernel, grid=(count,), in_specs=[pl.BlockSpec((1, units, t...  20.4 us
  transfers between devices with their start and end apart: 51, of which 21 were waited for; matrix products, arithmetic and copies ran while one was open for 12% of the time, Pallas kernels for 5%

profile of v1, /device:TPU:70, one launch (start us, length us, event | category | flops | bytes accessed | tf_op | source)
XLA Modules:
  0.0 423.6 jit_solution(1292146499285426419)
XLA Ops:
  6.4 5.8 %copy.86 = bf16[1,2,896,896]{2,3,1,0:T(8,128)(2,1)} copy(bf16[1,2,896,896]{3,2,1,0:T(8,128)(2,1)} %param.9) | data formatting | bytes 6422528 | tf_op args[4]
  12.2 3.8 fusion.16
  18.7 5.3 %collective-permute-start.32 = (bf16[112,896]{1,0:T(8,128)(2,1)}, bf16[112,896]{1,0:T(8,128)(2,1)}, u32[]{:S(2)}, u32[]{:S(2)}) collective-permute-start(bf16[112,896]{1,0:T(8,128)(2,1)} %get-tuple-element.25), channel_id=1, source_target_pairs={{0,112},{1,113},{2,114},{3,115},{4,116},{5,117},{6,118},{7,119},{8... | collective-permute-start | bytes 602120 | tf_op jit(solution)/shard_map/ppermute | solution.py:38
  31.3 4.3 %constant_dynamic-slice_fusion = (bf16[4096,112]{1,0:T(8,128)(2,1)}, bf16[4096,112]{1,0:T(8,128)(2,1)}) fusion(bf16[4096,896]{1,0:T(8,128)(2,1)} %param.6, s32[]{:T(128)S(6)} %select_n.107, bf16[4096,896]{1,0:T(8,128)(2,1)} %param.5), kind=kLoop, calls=%fused_computation.68 | loop fusion | bytes 3670020 | tf_op jit(solution)/shard_map/dynamic-slice.33
  47.5 28.3 %all_gather.3 = s32[8,2,896]{2,1,0:T(2,128)S(1)} all-gather(s32[1,2,896]{2,1,0:T(2,128)S(1)} %copy-done.31), channel_id=1, replica_groups=mesh['island'=8,'fsdp'=16] {'island'}, dimensions={0}, use_global_device_ids=true | all-gather | bytes 64512 | tf_op jit(solution)/shard_map/all_gather | solution.py:388
  81.9 4.9 %collective-permute-done.6 = bf16[384,256]{1,0:T(8,128)(2,1)S(1)} collective-permute-done((bf16[384,256]{1,0:T(8,128)(2,1)S(1)}, bf16[384,256]{1,0:T(8,128)(2,1)S(1)}, u32[]{:S(2)}, u32[]{:S(2)}) %collective-permute-start.6) | collective-permute-done | bytes 196640 | tf_op jit(solution)/shard_map/ppermute | solution.py:38
  90.1 4.2 collective-permute-done.27
  96.6 2.8 collective-permute-start.28
  99.5 6.5 %collective-permute-done.28 = bf16[112,896]{1,0:T(8,128)(2,1)S(1)} collective-permute-done((bf16[112,896]{1,0:T(8,128)(2,1)}, bf16[112,896]{1,0:T(8,128)(2,1)S(1)}, u32[]{:S(2)}, u32[]{:S(2)}) %collective-permute-start.28) | collective-permute-done | bytes 200736 | tf_op jit(solution)/shard_map/ppermute | solution.py:38
  109.4 15.2 %collective-permute-done.30 = bf16[112,896]{1,0:T(8,128)(2,1)S(1)} collective-permute-done((bf16[112,896]{1,0:T(8,128)(2,1)S(1)}, bf16[112,896]{1,0:T(8,128)(2,1)S(1)}, u32[]{:S(2)}, u32[]{:S(2)}) %collective-permute-start.30) | collective-permute-done | bytes 200736 | tf_op jit(solution)/shard_map/ppermute | solution.py:38
  124.6 5.7 %collective-permute-start.31 = (bf16[112,896]{1,0:T(8,128)(2,1)S(1)}, bf16[112,896]{1,0:T(8,128)(2,1)S(1)}, u32[]{:S(2)}, u32[]{:S(2)}) collective-permute-start(bf16[112,896]{1,0:T(8,128)(2,1)S(1)} %copy-done.22), channel_id=1, source_target_pairs={{0,96},{1,97},{2,98},{3,99},{4,100},{5,101},{6,102},{7,103},{8,104... | collective-permute-start | bytes 602120 | tf_op jit(solution)/shard_map/ppermute | solution.py:38
  131.3 2.8 collective-permute-start.24
  134.0 2.8 collective-permute-start.9
  151.5 15.8 %collective-permute-done.21 = bf16[112,896]{1,0:T(8,128)(2,1)S(1)} collective-permute-done((bf16[112,896]{1,0:T(8,128)(2,1)S(1)}, bf16[112,896]{1,0:T(8,128)(2,1)S(1)}, u32[]{:S(2)}, u32[]{:S(2)}) %collective-permute-start.21) | collective-permute-done | bytes 200736 | tf_op jit(solution)/shard_map/ppermute | solution.py:38
  169.8 3.4 collective-permute-done.19
  176.1 10.0 %collective-permute-done.4.refs_5_ = bf16[2560,256]{1,0:T(8,128)(2,1)S(1)} collective-permute-done((bf16[2560,256]{1,0:T(8,128)(2,1)S(1)}, bf16[2560,256]{1,0:T(8,128)(2,1)S(1)}, u32[]{:S(2)}, u32[]{:S(2)}) %collective-permute-start.4) | collective-permute-done | bytes 1310752 | tf_op jit(solution)/shard_map/ppermute | solution.py:38
  187.0 10.2 %add_by_row.2 = (bf16[8,64,2048]{2,1,0:T(8,128)(2,1)S(1)}, bf16[8,48,2048]{2,1,0:T(8,128)(2,1)S(1)}) custom-call(bf16[8,112,896]{2,1,0:T(8,128)(2,1)S(1)} %bitcast_dynamic-update-slice_fusion.7.cot_ref, s32[8,1,896]{2,1,0:T(1,128)S(1)} %constant_dynamic-update-slice_fusion.5.ids_ref), custom_call_target="tpu_custom_call" | custom-call | flops 3288334336 | bytes 5275648 | tf_op jit(solution)/shard_map/add_by_row/pallas_call | solution.py:162
  198.5 10.2 %add_by_row.3 = (bf16[8,64,2048]{2,1,0:T(8,128)(2,1)S(1)}, bf16[8,48,2048]{2,1,0:T(8,128)(2,1)S(1)}) custom-call(bf16[8,112,896]{2,1,0:T(8,128)(2,1)S(1)} %copy-done.12, s32[8,1,896]{2,1,0:T(1,128)S(1)} %constant_dynamic-update-slice_fusion.13.ids_ref), custom_call_target="tpu_custom_call" | custom-call | flops 3288334336 | bytes 5275648 | tf_op jit(solution)/shard_map/add_by_row/pallas_call | solution.py:162
  208.7 4.3 %gather_table.1.table_ref = bf16[2048,4096]{1,0:T(8,128)(2,1)S(1)} custom-call(s32[72,2]{1,0:T(8,128)S(1)} %stack.881.where_ref, bf16[2048,256]{1,0:T(8,128)(2,1)S(1)} %copy-done.1, bf16[1280,256]{1,0:T(8,128)(2,1)S(1)} %collective-permute-done.refs_1_, bf16[1280,256]{1,0:T(8,128)(2,1)S(1)} %collective-permute-done.1.refs_2_, ...), custom_call_target="tpu_custom_call" | custom-call | bytes 33554432 | tf_op jit(solution)/shard_map/gather_table/pallas_call | solution.py:134
  213.1 5.8 %copy-done = bf16[2048,4096]{1,0:T(8,128)(2,1)} copy-done((bf16[2048,4096]{1,0:T(8,128)(2,1)}, bf16[2048,4096]{1,0:T(8,128)(2,1)S(1)}, u32[]{:S(2)}) %copy-start) | copy-done | bytes 16777240
  221.5 24.4 %first_step.2 = (bf16[512,4096]{1,0:T(8,128)(2,1)S(1)}, bf16[512,4096]{1,0:T(8,128)(2,1)S(1)}) custom-call(bf16[2048,4096]{1,0:T(8,128)(2,1)} %copy-done, bf16[64,4096]{1,0:T(8,128)(2,1)S(1)} %copy-done.5, bf16[8,64,2048]{2,1,0:T(8,128)(2,1)S(1)} %copy-done.21, bf16[64,4096]{1,0:T(8,128)(2,1)S(1)} %copy-done.5), custom_call_target="tpu_custom_call" | custom-call | flops 9663676416 | bytes 26214400 | tf_op jit(solution)/shard_map/first_step/pallas_call | solution.py:210
  246.0 16.9 %second_upstream.2.up_ref = bf16[512,2048]{1,0:T(8,128)(2,1)S(1)} custom-call(bf16[2048,4096]{1,0:T(8,128)(2,1)} %copy-done, bf16[512,4096]{1,0:T(8,128)(2,1)S(1)} %get-tuple-element.14.work_ref, bf16[512,2048]{1,0:T(8,128)(2,1)S(1)} %bitcast.237), custom_call_target="tpu_custom_call" | custom-call | flops 8589934592 | bytes 20971520 | tf_op jit(solution)/shard_map/second_upstream/pallas_call | solution.py:243
  263.0 35.1 %outer_step.2 = bf16[64,4096]{1,0:T(8,128)(2,1)S(1)} custom-call(bf16[2048,4096]{1,0:T(8,128)(2,1)} %copy-done, bf16[512,2048]{1,0:T(8,128)(2,1)S(1)} %second_upstream.2.up_ref, bf16[512,4096]{1,0:T(8,128)(2,1)S(1)} %get-tuple-element.16.grad_ref, bf16[64,4096]{1,0:T(8,128)(2,1)S(1)} %copy-done.6, bf16[64,4096]{1,0:T(8,128)(2,1)S(1)} %copy-done.4), custom_call_target="tpu_custom_call" | custom-call | flops 8589934592 | bytes 26214400 | tf_op jit(solution)/shard_map/outer_step/pallas_call | solution.py:287
  298.1 21.3 %first_step.3 = (bf16[384,4096]{1,0:T(8,128)(2,1)S(1)}, bf16[384,4096]{1,0:T(8,128)(2,1)S(1)}) custom-call(bf16[2048,4096]{1,0:T(8,128)(2,1)} %copy-done, bf16[48,4096]{1,0:T(8,128)(2,1)S(1)} %copy-done.10, bf16[8,48,2048]{2,1,0:T(8,128)(2,1)S(1)} %copy-done.19, bf16[48,4096]{1,0:T(8,128)(2,1)S(1)} %copy-done.10), custom_call_target="tpu_custom_call" | custom-call | flops 7247757312 | bytes 23855104 | tf_op jit(solution)/shard_map/first_step/pallas_call | solution.py:210
  319.5 14.3 %second_upstream.3.up_ref = bf16[384,2048]{1,0:T(8,128)(2,1)S(1)} custom-call(bf16[2048,4096]{1,0:T(8,128)(2,1)} %copy-done, bf16[384,4096]{1,0:T(8,128)(2,1)S(1)} %get-tuple-element.18.work_ref, bf16[384,2048]{1,0:T(8,128)(2,1)S(1)} %bitcast.238), custom_call_target="tpu_custom_call" | custom-call | flops 6442450944 | bytes 19922944 | tf_op jit(solution)/shard_map/second_upstream/pallas_call | solution.py:243
  333.8 21.5 %outer_step.3 = bf16[48,4096]{1,0:T(8,128)(2,1)S(1)} custom-call(bf16[2048,4096]{1,0:T(8,128)(2,1)} %copy-done, bf16[384,2048]{1,0:T(8,128)(2,1)S(1)} %second_upstream.3.up_ref, bf16[384,4096]{1,0:T(8,128)(2,1)S(1)} %get-tuple-element.20.grad_ref, bf16[48,4096]{1,0:T(8,128)(2,1)S(1)} %copy-done.10, bf16[48,4096]{1,0:T(8,128)(2,1)S(1)} %copy-done.9), custom_call_target="tpu_custom_call" | custom-call | flops 6442450944 | bytes 23855104 | tf_op jit(solution)/shard_map/outer_step/pallas_call | solution.py:287
  362.2 5.7 %collective-permute-done.45.refs_17_ = bf16[48,1408]{1,0:T(8,128)(2,1)S(1)} collective-permute-done((bf16[48,1408]{1,0:T(8,128)(2,1)S(1)}, bf16[48,1408]{1,0:T(8,128)(2,1)S(1)}, u32[]{:S(2)}, u32[]{:S(2)}) %collective-permute-start.45) | collective-permute-done | bytes 135200 | tf_op jit(solution)/shard_map/ppermute | solution.py:38
  373.6 3.3 collective-permute-done.49.refs_22_
  385.8 3.6 collective-permute-done.34.refs_2_
  391.7 8.3 %collective-permute-done.50.refs_23_ = bf16[192,1280]{1,0:T(8,128)(2,1)S(1)} collective-permute-done((bf16[192,1280]{1,0:T(8,128)(2,1)S(1)}, bf16[192,1280]{1,0:T(8,128)(2,1)S(1)}, u32[]{:S(2)}, u32[]{:S(2)}) %collective-permute-start.50) | collective-permute-done | bytes 491552 | tf_op jit(solution)/shard_map/ppermute | solution.py:38
  401.4 13.7 %collective-permute-done.44.refs_15_ = bf16[192,1408]{1,0:T(8,128)(2,1)} collective-permute-done((bf16[192,1408]{1,0:T(8,128)(2,1)}, bf16[192,1408]{1,0:T(8,128)(2,1)}, u32[]{:S(2)}, u32[]{:S(2)}) %collective-permute-start.44) | collective-permute-done | bytes 540704 | tf_op jit(solution)/shard_map/ppermute | solution.py:38
  417.0 6.3 %assemble.1 = bf16[4096,896]{1,0:T(8,128)(2,1)} custom-call(s32[8]{0:T(128)S(1)} %stack.714.where_ref, bf16[64,1408]{1,0:T(8,128)(2,1)S(1)} %get-tuple-element.42.refs_0_, bf16[64,1408]{1,0:T(8,128)(2,1)S(1)} %collective-permute-done.33.refs_1_, bf16[128,1408]{1,0:T(8,128)(2,1)S(1)} %collective-permute-done.34.refs_2_, ...), custom_call_target="tpu_custom_call" | custom-call | bytes 14680064 | tf_op jit(solution)/shard_map/assemble/pallas_call | solution.py:363
  (281 shorter events, 95.9 us)
Async XLA Ops:
  2.0 132.0 %collective-permute-start.1 = (bf16[1280,256]{1,0:T(8,128)(2,1)}, bf16[1280,256]{1,0:T(8,128)(2,1)S(1)}, u32[]{:S(2)}, u32[]{:S(2)}) collective-permute-start(bf16[1280,256]{1,0:T(8,128)(2,1)} %slice.30), channel_id=1, source_target_pairs={{0,2},{1,7},{2,0},{3,5},{4,6},{5,3},{6,4},{7,1},{8,10},{9,15},{10,... | collective-permute-start | bytes 1966088 | tf_op jit(solution)/shard_map/ppermute | solution.py:38
  2.8 127.5 %collective-permute-start = (bf16[1280,256]{1,0:T(8,128)(2,1)}, bf16[1280,256]{1,0:T(8,128)(2,1)S(1)}, u32[]{:S(2)}, u32[]{:S(2)}) collective-permute-start(bf16[1280,256]{1,0:T(8,128)(2,1)} %slice.30), channel_id=1, source_target_pairs={{0,72},{1,73},{2,74},{3,75},{4,76},{5,77},{6,78},{7,79},{8,64},{9,... | collective-permute-start | bytes 1966088 | tf_op jit(solution)/shard_map/ppermute | solution.py:38
  4.5 75.4 %collective-permute-start.5 = (bf16[192,256]{1,0:T(8,128)(2,1)S(1)}, bf16[192,256]{1,0:T(8,128)(2,1)S(1)}, u32[]{:S(2)}, u32[]{:S(2)}) collective-permute-start(bf16[192,256]{1,0:T(8,128)(2,1)S(1)} %get-tuple-element.22), channel_id=1, source_target_pairs={{0,72},{1,73},{2,74},{3,75},{4,76},{5,77},{6,78},{7,79},{8,64},{9,... | collective-permute-start | bytes 294920 | tf_op jit(solution)/shard_map/ppermute | solution.py:38
  18.7 112.6 %collective-permute-start.32 = (bf16[112,896]{1,0:T(8,128)(2,1)}, bf16[112,896]{1,0:T(8,128)(2,1)}, u32[]{:S(2)}, u32[]{:S(2)}) collective-permute-start(bf16[112,896]{1,0:T(8,128)(2,1)} %get-tuple-element.25), channel_id=1, source_target_pairs={{0,112},{1,113},{2,114},{3,115},{4,116},{5,117},{6,118},{7,119},{8... | collective-permute-start | bytes 602120 | tf_op jit(solution)/shard_map/ppermute | solution.py:38
  24.0 63.6 %collective-permute-start.26 = (bf16[112,896]{1,0:T(8,128)(2,1)}, bf16[112,896]{1,0:T(8,128)(2,1)}, u32[]{:S(2)}, u32[]{:S(2)}) collective-permute-start(bf16[112,896]{1,0:T(8,128)(2,1)} %get-tuple-element.31), channel_id=1, source_target_pairs={{0,16},{1,17},{2,18},{3,19},{4,20},{5,21},{6,22},{7,23},{8,24},{9,... | collective-permute-start | bytes 602120 | tf_op jit(solution)/shard_map/ppermute | solution.py:38
  94.3 12.7 %collective-permute-start.29 = (bf16[112,896]{1,0:T(8,128)(2,1)}, bf16[112,896]{1,0:T(8,128)(2,1)S(1)}, u32[]{:S(2)}, u32[]{:S(2)}) collective-permute-start(bf16[112,896]{1,0:T(8,128)(2,1)} %get-tuple-element.28), channel_id=1, source_target_pairs={{0,64},{1,65},{2,66},{3,67},{4,68},{5,69},{6,70},{7,71},{8,72},{9,... | collective-permute-start | bytes 602120 | tf_op jit(solution)/shard_map/ppermute | solution.py:38
  106.0 25.0 %collective-permute-start.8 = (bf16[1536,256]{1,0:T(8,128)(2,1)S(1)}, bf16[1536,256]{1,0:T(8,128)(2,1)S(1)}, u32[]{:S(2)}, u32[]{:S(2)}) collective-permute-start(bf16[1536,256]{1,0:T(8,128)(2,1)S(1)} %pad_maximum_fusion.2.refs_6_), channel_id=1, source_target_pairs={{0,16},{1,49},{2,18},{3,51},{4,20},{5,53},{6,22},{7,55},{8,24},{9,... | collective-permute-start | bytes 2359304 | tf_op jit(solution)/shard_map/ppermute | solution.py:38
  107.1 17.5 %collective-permute-start.30 = (bf16[112,896]{1,0:T(8,128)(2,1)S(1)}, bf16[112,896]{1,0:T(8,128)(2,1)S(1)}, u32[]{:S(2)}, u32[]{:S(2)}) collective-permute-start(bf16[112,896]{1,0:T(8,128)(2,1)S(1)} %copy-done.23), channel_id=1, source_target_pairs={{0,80},{1,81},{2,82},{3,83},{4,84},{5,85},{6,86},{7,87},{8,88},{9,... | collective-permute-start | bytes 602120 | tf_op jit(solution)/shard_map/ppermute | solution.py:38
  124.6 13.4 %collective-permute-start.31 = (bf16[112,896]{1,0:T(8,128)(2,1)S(1)}, bf16[112,896]{1,0:T(8,128)(2,1)S(1)}, u32[]{:S(2)}, u32[]{:S(2)}) collective-permute-start(bf16[112,896]{1,0:T(8,128)(2,1)S(1)} %copy-done.22), channel_id=1, source_target_pairs={{0,96},{1,97},{2,98},{3,99},{4,100},{5,101},{6,102},{7,103},{8,104... | collective-permute-start | bytes 602120 | tf_op jit(solution)/shard_map/ppermute | solution.py:38
  130.4 13.8 %collective-permute-start.2 = (bf16[1280,256]{1,0:T(8,128)(2,1)S(1)}, bf16[1280,256]{1,0:T(8,128)(2,1)S(1)}, u32[]{:S(2)}, u32[]{:S(2)}) collective-permute-start(bf16[1280,256]{1,0:T(8,128)(2,1)S(1)} %collective-permute-done.refs_1_), channel_id=1, source_target_pairs={{0,2},{1,7},{2,0},{3,5},{4,6},{5,3},{6,4},{7,1},{8,10},{9,15},{10,... | collective-permute-start | bytes 1966088 | tf_op jit(solution)/shard_map/ppermute | solution.py:38
  134.0 40.1 %collective-permute-start.9 = (bf16[3072,256]{1,0:T(8,128)(2,1)S(1)}, bf16[3072,256]{1,0:T(8,128)(2,1)S(1)}, u32[]{:S(2)}, u32[]{:S(2)}) collective-permute-start(bf16[3072,256]{1,0:T(8,128)(2,1)S(1)} %constant_dynamic-update-slice_fusion), channel_id=1, source_target_pairs={{0,48},{1,17},{2,50},{3,19},{4,52},{5,21},{6,54},{7,23},{8,56},{9,... | collective-permute-start | bytes 4718600 | tf_op jit(solution)/shard_map/ppermute | solution.py:38
  138.0 35.5 %collective-permute-start.10 = (bf16[2048,256]{1,0:T(8,128)(2,1)S(1)}, bf16[2048,256]{1,0:T(8,128)(2,1)S(1)}, u32[]{:S(2)}, u32[]{:S(2)}) collective-permute-start(bf16[2048,256]{1,0:T(8,128)(2,1)S(1)} %copy-done.1), channel_id=1, source_target_pairs={{0,1},{1,0},{2,3},{3,2},{4,5},{5,4},{6,7},{7,6},{8,9},{9,8},{10,11... | collective-permute-start | bytes 3145736 | tf_op jit(solution)/shard_map/ppermute | solution.py:38
  144.1 23.2 %collective-permute-start.21 = (bf16[112,896]{1,0:T(8,128)(2,1)S(1)}, bf16[112,896]{1,0:T(8,128)(2,1)S(1)}, u32[]{:S(2)}, u32[]{:S(2)}) collective-permute-start(bf16[112,896]{1,0:T(8,128)(2,1)S(1)} %copy-done.26), channel_id=1, source_target_pairs={{0,48},{1,49},{2,50},{3,51},{4,52},{5,53},{6,54},{7,55},{8,56},{9,... | collective-permute-start | bytes 602120 | tf_op jit(solution)/shard_map/ppermute | solution.py:38
  149.1 18.3 %collective-permute-start.20 = (bf16[112,896]{1,0:T(8,128)(2,1)S(1)}, bf16[112,896]{1,0:T(8,128)(2,1)S(1)}, u32[]{:S(2)}, u32[]{:S(2)}) collective-permute-start(bf16[112,896]{1,0:T(8,128)(2,1)S(1)} %copy-done.25), channel_id=1, source_target_pairs={{0,32},{1,33},{2,34},{3,35},{4,36},{5,37},{6,38},{7,39},{8,40},{9,... | collective-permute-start | bytes 602120 | tf_op jit(solution)/shard_map/ppermute | solution.py:38
  151.1 24.6 %collective-permute-start.3 = (bf16[2560,256]{1,0:T(8,128)(2,1)S(1)}, bf16[2560,256]{1,0:T(8,128)(2,1)S(1)}, u32[]{:S(2)}, u32[]{:S(2)}) collective-permute-start(bf16[2560,256]{1,0:T(8,128)(2,1)S(1)} %pad_maximum_fusion), channel_id=1, source_target_pairs={{0,6},{1,3},{2,4},{3,1},{4,2},{5,7},{6,0},{7,5},{8,14},{9,11},{10,... | collective-permute-start | bytes 3932168 | tf_op jit(solution)/shard_map/ppermute | solution.py:38
  167.3 18.8 %collective-permute-start.4 = (bf16[2560,256]{1,0:T(8,128)(2,1)S(1)}, bf16[2560,256]{1,0:T(8,128)(2,1)S(1)}, u32[]{:S(2)}, u32[]{:S(2)}) collective-permute-start(bf16[2560,256]{1,0:T(8,128)(2,1)S(1)} %pad_maximum_fusion.1), channel_id=1, source_target_pairs={{0,6},{1,3},{2,4},{3,1},{4,2},{5,7},{6,0},{7,5},{8,14},{9,11},{10,... | collective-permute-start | bytes 3932168 | tf_op jit(solution)/shard_map/ppermute | solution.py:38
  173.5 13.3 %collective-permute-start.16 = (bf16[1536,256]{1,0:T(8,128)(2,1)S(1)}, bf16[1536,256]{1,0:T(8,128)(2,1)S(1)}, u32[]{:S(2)}, u32[]{:S(2)}) collective-permute-start(bf16[1536,256]{1,0:T(8,128)(2,1)S(1)} %pad_maximum_fusion.2.refs_6_), channel_id=1, source_target_pairs={{0,1},{1,0},{2,3},{3,2},{4,5},{5,4},{6,7},{7,6},{8,9},{9,8},{10,11... | collective-permute-start | bytes 2359304 | tf_op jit(solution)/shard_map/ppermute | solution.py:38
  174.1 34.7 %collective-permute-start.18 = (bf16[3072,256]{1,0:T(8,128)(2,1)S(1)}, bf16[3072,256]{1,0:T(8,128)(2,1)S(1)}, u32[]{:S(2)}, u32[]{:S(2)}) collective-permute-start(bf16[3072,256]{1,0:T(8,128)(2,1)S(1)} %collective-permute-done.9.refs_8_), channel_id=1, source_target_pairs={{0,1},{1,0},{2,3},{3,2},{4,5},{5,4},{6,7},{7,6},{8,9},{9,8},{10,11... | collective-permute-start | bytes 4718600 | tf_op jit(solution)/shard_map/ppermute | solution.py:38
  175.7 33.0 %collective-permute-start.14 = (bf16[2560,256]{1,0:T(8,128)(2,1)S(1)}, bf16[2560,256]{1,0:T(8,128)(2,1)S(1)}, u32[]{:S(2)}, u32[]{:S(2)}) collective-permute-start(bf16[2560,256]{1,0:T(8,128)(2,1)S(1)} %collective-permute-done.3.refs_4_), channel_id=1, source_target_pairs={{0,1},{1,0},{2,3},{3,2},{4,5},{5,4},{6,7},{7,6},{8,9},{9,8},{10,11... | collective-permute-start | bytes 3932168 | tf_op jit(solution)/shard_map/ppermute | solution.py:38
  186.2 22.6 %collective-permute-start.15 = (bf16[2560,256]{1,0:T(8,128)(2,1)S(1)}, bf16[2560,256]{1,0:T(8,128)(2,1)S(1)}, u32[]{:S(2)}, u32[]{:S(2)}) collective-permute-start(bf16[2560,256]{1,0:T(8,128)(2,1)S(1)} %collective-permute-done.4.refs_5_), channel_id=1, source_target_pairs={{0,1},{1,0},{2,3},{3,2},{4,5},{5,4},{6,7},{7,6},{8,9},{9,8},{10,11... | collective-permute-start | bytes 3932168 | tf_op jit(solution)/shard_map/ppermute | solution.py:38
  186.2 22.5 %collective-permute-start.13 = (bf16[1280,256]{1,0:T(8,128)(2,1)S(1)}, bf16[1280,256]{1,0:T(8,128)(2,1)S(1)}, u32[]{:S(2)}, u32[]{:S(2)}) collective-permute-start(bf16[1280,256]{1,0:T(8,128)(2,1)S(1)} %collective-permute-done.2.refs_3_), channel_id=1, source_target_pairs={{0,1},{1,0},{2,3},{3,2},{4,5},{5,4},{6,7},{7,6},{8,9},{9,8},{10,11... | collective-permute-start | bytes 1966088 | tf_op jit(solution)/shard_map/ppermute | solution.py:38
  186.8 21.9 %collective-permute-start.17 = (bf16[1536,256]{1,0:T(8,128)(2,1)S(1)}, bf16[1536,256]{1,0:T(8,128)(2,1)S(1)}, u32[]{:S(2)}, u32[]{:S(2)}) collective-permute-start(bf16[1536,256]{1,0:T(8,128)(2,1)S(1)} %collective-permute-done.8.refs_7_), channel_id=1, source_target_pairs={{0,1},{1,0},{2,3},{3,2},{4,5},{5,4},{6,7},{7,6},{8,9},{9,8},{10,11... | collective-permute-start | bytes 2359304 | tf_op jit(solution)/shard_map/ppermute | solution.py:38
  355.9 13.5 %collective-permute-start.39 = (bf16[64,1280]{1,0:T(8,128)(2,1)S(1)}, bf16[64,1280]{1,0:T(8,128)(2,1)S(1)}, u32[]{:S(2)}, u32[]{:S(2)}) collective-permute-start(bf16[64,1280]{1,0:T(8,128)(2,1)S(1)} %slice.96.refs_8_), channel_id=1, source_target_pairs={{0,64},{1,65},{2,66},{3,67},{4,68},{5,69},{6,70},{7,71},{8,72},{9,... | collective-permute-start | bytes 491528 | tf_op jit(solution)/shard_map/ppermute | solution.py:38
  357.5 13.6 %collective-permute-start.36 = (bf16[64,1408]{1,0:T(8,128)(2,1)S(1)}, bf16[64,1408]{1,0:T(8,128)(2,1)S(1)}, u32[]{:S(2)}, u32[]{:S(2)}) collective-permute-start(bf16[64,1408]{1,0:T(8,128)(2,1)S(1)} %get-tuple-element.41.refs_4_), channel_id=1, source_target_pairs={{0,48},{1,49},{2,50},{3,51},{4,52},{5,53},{6,54},{7,55},{8,56},{9,... | collective-permute-start | bytes 540680 | tf_op jit(solution)/shard_map/ppermute | solution.py:38
  359.0 13.7 %collective-permute-start.33 = (bf16[64,1408]{1,0:T(8,128)(2,1)S(1)}, bf16[64,1408]{1,0:T(8,128)(2,1)S(1)}, u32[]{:S(2)}, u32[]{:S(2)}) collective-permute-start(bf16[64,1408]{1,0:T(8,128)(2,1)S(1)} %get-tuple-element.42.refs_0_), channel_id=1, source_target_pairs={{0,16},{1,17},{2,18},{3,19},{4,20},{5,21},{6,22},{7,23},{8,24},{9,... | collective-permute-start | bytes 540680 | tf_op jit(solution)/shard_map/ppermute | solution.py:38
  369.4 20.9 %collective-permute-start.43 = (bf16[96,1408]{1,0:T(8,128)(2,1)S(1)}, bf16[96,1408]{1,0:T(8,128)(2,1)S(1)}, u32[]{:S(2)}, u32[]{:S(2)}) collective-permute-start(bf16[96,1408]{1,0:T(8,128)(2,1)S(1)} %pad_maximum_fusion.13), channel_id=1, source_target_pairs={{0,48},{1,49},{2,50},{3,51},{4,52},{5,53},{6,54},{7,55},{8,56},{9,... | collective-permute-start | bytes 811016 | tf_op jit(solution)/shard_map/ppermute | solution.py:38
  378.4 21.6 %collective-permute-start.50 = (bf16[192,1280]{1,0:T(8,128)(2,1)S(1)}, bf16[192,1280]{1,0:T(8,128)(2,1)S(1)}, u32[]{:S(2)}, u32[]{:S(2)}) collective-permute-start(bf16[192,1280]{1,0:T(8,128)(2,1)S(1)} %pad_maximum_fusion.8), channel_id=1, source_target_pairs={{0,48},{1,49},{2,50},{3,51},{4,52},{5,53},{6,54},{7,55},{8,56},{9,... | collective-permute-start | bytes 1474568 | tf_op jit(solution)/shard_map/ppermute | solution.py:38
  381.9 19.5 %collective-permute-start.47 = (bf16[192,1408]{1,0:T(8,128)(2,1)}, bf16[192,1408]{1,0:T(8,128)(2,1)}, u32[]{:S(2)}, u32[]{:S(2)}) collective-permute-start(bf16[192,1408]{1,0:T(8,128)(2,1)} %pad_maximum_fusion.7), channel_id=1, source_target_pairs={{0,16},{1,17},{2,18},{3,19},{4,20},{5,21},{6,22},{7,23},{8,24},{9,... | collective-permute-start | bytes 1622024 | tf_op jit(solution)/shard_map/ppermute | solution.py:38
  383.4 31.6 %collective-permute-start.41 = (bf16[256,1280]{1,0:T(8,128)(2,1)}, bf16[256,1280]{1,0:T(8,128)(2,1)}, u32[]{:S(2)}, u32[]{:S(2)}) collective-permute-start(bf16[256,1280]{1,0:T(8,128)(2,1)} %pad_maximum_fusion.5), channel_id=1, source_target_pairs={{0,48},{1,49},{2,50},{3,51},{4,52},{5,53},{6,54},{7,55},{8,56},{9,... | collective-permute-start | bytes 1966088 | tf_op jit(solution)/shard_map/ppermute | solution.py:38
  389.4 25.6 %collective-permute-start.38 = (bf16[256,1408]{1,0:T(8,128)(2,1)}, bf16[256,1408]{1,0:T(8,128)(2,1)}, u32[]{:S(2)}, u32[]{:S(2)}) collective-permute-start(bf16[256,1408]{1,0:T(8,128)(2,1)} %pad_maximum_fusion.4), channel_id=1, source_target_pairs={{0,16},{1,17},{2,18},{3,19},{4,20},{5,21},{6,22},{7,23},{8,24},{9,... | collective-permute-start | bytes 2162696 | tf_op jit(solution)/shard_map/ppermute | solution.py:38
  390.3 24.7 %collective-permute-start.35 = (bf16[256,1408]{1,0:T(8,128)(2,1)}, bf16[256,1408]{1,0:T(8,128)(2,1)}, u32[]{:S(2)}, u32[]{:S(2)}) collective-permute-start(bf16[256,1408]{1,0:T(8,128)(2,1)} %pad_maximum_fusion.3), channel_id=1, source_target_pairs={{0,64},{1,65},{2,66},{3,67},{4,68},{5,69},{6,70},{7,71},{8,72},{9,... | collective-permute-start | bytes 2162696 | tf_op jit(solution)/shard_map/ppermute | solution.py:38
  400.8 14.3 %collective-permute-start.44 = (bf16[192,1408]{1,0:T(8,128)(2,1)}, bf16[192,1408]{1,0:T(8,128)(2,1)}, u32[]{:S(2)}, u32[]{:S(2)}) collective-permute-start(bf16[192,1408]{1,0:T(8,128)(2,1)} %pad_maximum_fusion.6), channel_id=1, source_target_pairs={{0,64},{1,65},{2,66},{3,67},{4,68},{5,69},{6,70},{7,71},{8,72},{9,... | collective-permute-start | bytes 1622024 | tf_op jit(solution)/shard_map/ppermute | solution.py:38
  (66 other events, 686.9 us)

commit v2 on v0

v2 whole, which is shorter than its diff:
```python
import math

import jax
import jax.numpy as jnp
from jax import lax
from jax.experimental import pallas as pl
from jax.experimental.pallas import tpu as pltpu
from jax.sharding import PartitionSpec as P

beta_one = 0.9
beta_two = 0.95
adam_eps = 0.0001
inner_rate = 0.1
decay_rate = 0.1
outer_rate = 0.7
outer_moment = 0.9

MB = 1 << 20
AXES = ("island", "fsdp")
XA, XB = 1, 3
DIRECT = 768
PARTS = ((0, 1408), (1408, 1408), (2816, 1280))
ORDERS = ((1, 3, 4), (3, 4, 1), (4, 1, 3))
IDS = 16


def small(**kw):
    return pl.CostEstimate(flops=0, bytes_accessed=1024, transcendentals=0)


def swap(a, partner):
    pairs = []
    for zlo in range(2):
        for y in range(4):
            for zhi in range(2):
                for x in range(4):
                    for c in range(2):
                        px, py, pz, pc = partner(x, y, zhi * 2 + zlo, c)
                        me = (zlo * 4 + y) * 16 + zhi * 8 + x * 2 + c
                        to = ((pz % 2) * 4 + py) * 16 + (pz // 2) * 8 + px * 2 + pc
                        pairs.append((me, to))
    return lax.ppermute(a, AXES, pairs)


def over_x(a, first):
    return swap(a, lambda x, y, z, c: (x ^ (XA if (c == 0) == first else XB), y, z, c))


def over_y(a, first):
    return swap(a, lambda x, y, z, c: (x, y ^ (XA if (c == 0) == first else XB), z, c))


def over_z(a):
    return swap(a, lambda x, y, z, c: (x, y, z ^ 3, c))


def over_core(a):
    return swap(a, lambda x, y, z, c: (x, y, z, c ^ 1))


def over_island(a, mask):
    return swap(a, lambda x, y, z, c: (x, y ^ (mask & 3), z ^ (mask >> 2), c))


def slope(hidden):
    sigma = 0.5 * (1.0 + jnp.tanh(0.5 * hidden))
    return sigma * (1.0 + hidden * (1.0 - sigma))


def turn_cotangent(cot, ids, island):
    steps, tokens, hidden_units = cot.shape
    units = hidden_units // 8
    where = ((island ^ jnp.arange(8)) * units).astype(jnp.int32)

    def kernel(where_ref, cot_ref, ids_ref, *refs):
        outs, held, turned, digits, in_sems, out_sems = refs[:8], refs[8], refs[9], refs[10], refs[11], refs[12]
        loads = []
        for s in range(steps):
            load = pltpu.make_async_copy(cot_ref.at[s], held.at[s], in_sems.at[s])
            load.start()
            loads.append(load)
        row = lax.broadcasted_iota(jnp.int32, (IDS, tokens), 0)
        rows = jnp.zeros((IDS, tokens), jnp.int32)
        for s in range(steps):
            one = ids_ref[s : s + 1, :]
            rows = jnp.where(row == 2 * s, one >> 8, jnp.where(row == 2 * s + 1, one & 255, rows))
        digits[...] = rows.astype(jnp.float32).astype(jnp.bfloat16)
        stores = []

        def store(source, target, k):
            copy = pltpu.make_async_copy(source, target, out_sems.at[k])
            copy.start()
            stores.append(copy)

        for m in range(8):
            store(digits, outs[m].at[pl.ds(steps * units, IDS), :], 16 + m)
        for s in range(steps):
            loads[s].wait()
            for col in range(0, hidden_units, 128):
                turned[s, col : col + 128, :] = held[s, :, col : col + 128].T
            for m in range(8):
                at = pl.multiple_of(where_ref[m], 16)
                store(turned.at[s, pl.ds(at, units), :], outs[m].at[pl.ds(s * units, units), :], 8 * s + m)
        for copy in stores:
            copy.wait()

    return pl.pallas_call(
        kernel,
        in_specs=[
            pl.BlockSpec(memory_space=pltpu.SMEM),
            pl.BlockSpec(memory_space=pltpu.HBM),
            pl.BlockSpec(memory_space=pltpu.VMEM),
        ],
        out_specs=[pl.BlockSpec(memory_space=pltpu.HBM)] * 8,
        out_shape=[jax.ShapeDtypeStruct((steps * units + IDS, tokens), cot.dtype)] * 8,
        scratch_shapes=[
            pltpu.VMEM((steps, tokens, hidden_units), cot.dtype),
            pltpu.VMEM((steps, hidden_units, tokens), cot.dtype),
            pltpu.VMEM((IDS, tokens), cot.dtype),
            pltpu.SemaphoreType.DMA((steps,)),
            pltpu.SemaphoreType.DMA((24,)),
        ],
        compiler_params=pltpu.CompilerParams(vmem_limit_bytes=60 * MB),
        cost_estimate=small(),
        name="turn_cotangent",
    )(where, cot, ids)


def own_rows(weights, momentum, island, after):
    width, hidden_units = weights.shape
    units = hidden_units // 8
    first = island * units
    low = jnp.minimum(first // 128, hidden_units // 128 - 2) * 128
    where = jnp.stack([low, first - low]).astype(jnp.int32)

    def kernel(where_ref, w_ref, m_ref, _, w_out, m_out, held, turned, sems):
        cols = pl.ds(pl.multiple_of(where_ref[0], 128), 256)
        rows = pl.ds(pl.multiple_of(where_ref[1], 16), units)
        loads = []
        for k, ref in enumerate((w_ref, m_ref)):
            load = pltpu.make_async_copy(ref.at[:, cols], held.at[k], sems.at[k])
            load.start()
            loads.append(load)
        for k, out in enumerate((w_out, m_out)):
            loads[k].wait()
            for at in range(0, width, 512):
                turned[:, at : at + 512] = held[k, at : at + 512, :].T
            out[...] = turned[rows, :]

    return pl.pallas_call(
        kernel,
        in_specs=[pl.BlockSpec(memory_space=pltpu.SMEM)] + [pl.BlockSpec(memory_space=pltpu.HBM)] * 3,
        out_specs=[pl.BlockSpec(memory_space=pltpu.VMEM)] * 2,
        out_shape=[jax.ShapeDtypeStruct((units, width), weights.dtype)] * 2,
        scratch_shapes=[
            pltpu.VMEM((2, width, 256), weights.dtype),
            pltpu.VMEM((256, width), weights.dtype),
            pltpu.SemaphoreType.DMA((2,)),
        ],
        compiler_params=pltpu.CompilerParams(vmem_limit_bytes=60 * MB),
        cost_estimate=small(),
        name="own_rows",
    )(where, weights, momentum, after)


def add_by_row(arrived, rows, step, steps, after):
    tokens = arrived[0].shape[1]
    units = (arrived[0].shape[0] - IDS) // steps
    highs = rows // 256

    def kernel(*refs):
        messages, out = refs[:8], refs[9]
        row = lax.broadcasted_iota(jnp.int32, (256, tokens), 0).astype(jnp.float32)
        for m in range(8):
            digits = messages[m][steps * units : steps * units + IDS, :].astype(jnp.float32)
            high, low = digits[2 * step : 2 * step + 1], digits[2 * step + 1 : 2 * step + 2]
            hot = jnp.where(low == row, 1.0, 0.0).astype(jnp.bfloat16)
            cot = messages[m][step * units : (step + 1) * units, :]
            parted = [cot * jnp.where(high == float(k), 1.0, 0.0).astype(jnp.bfloat16) for k in range(highs)]
            total = lax.dot_general(
                jnp.concatenate(parted), hot, (((1,), (1,)), ((), ())), preferred_element_type=jnp.float32
            ).astype(jnp.bfloat16)
            for k in range(highs):
                out[m * units : (m + 1) * units, k * 256 : (k + 1) * 256] = total[k * units : (k + 1) * units]

    return pl.pallas_call(
        kernel,
        in_specs=[pl.BlockSpec(memory_space=pltpu.VMEM)] * 8 + [pl.BlockSpec(memory_space=pltpu.HBM)],
        out_specs=pl.BlockSpec(memory_space=pltpu.VMEM),
        out_shape=jax.ShapeDtypeStruct((8 * units, rows), jnp.bfloat16),
        compiler_params=pltpu.CompilerParams(vmem_limit_bytes=24 * MB),
        cost_estimate=pl.CostEstimate(flops=4 * 10**9, bytes_accessed=7 * MB, transcendentals=0),
        name="add_by_row",
    )(*arrived, after)


def pack(pieces, after=()):
    total = sum(count for _, _, count in pieces)
    width = pieces[0][0].shape[1]
    firsts = jnp.stack([jnp.asarray(low, jnp.int32) for _, low, _ in pieces])
    n = len(pieces)

    def kernel(firsts_ref, *refs):
        out, sems = refs[n + len(after)], refs[n + len(after) + 1]
        copies, at = [], 0
        for k, (_, _, count) in enumerate(pieces):
            low = pl.multiple_of(firsts_ref[k], 16)
            copy = pltpu.make_async_copy(refs[k].at[pl.ds(low, count), :], out.at[pl.ds(at, count), :], sems.at[k])
            copy.start()
            copies.append(copy)
            at += count
        for copy in copies:
            copy.wait()

    return pl.pallas_call(
        kernel,
        in_specs=[pl.BlockSpec(memory_space=pltpu.SMEM)] + [pl.BlockSpec(memory_space=pltpu.HBM)] * (n + len(after)),
        out_specs=pl.BlockSpec(memory_space=pltpu.VMEM),
        out_shape=jax.ShapeDtypeStruct((total, width), pieces[0][0].dtype),
        scratch_shapes=[pltpu.SemaphoreType.DMA((n,))],
        compiler_params=pltpu.CompilerParams(vmem_limit_bytes=8 * MB),
        cost_estimate=small(),
        name="pack",
    )(firsts, *(array for array, _, _ in pieces), *after)


def gather_pieces(table, messages, island, beside):
    rows = table.shape[0]
    odd = island % 2
    half, left = rows // 2, (rows - DIRECT) // 2
    z = over_z(table)
    x1 = over_x(table, True)
    table_o = over_core(table)
    send = pack([(table, odd * half, half), (x1, odd * half, half)], messages[1:2])
    x2 = over_x(send, False)
    x1_o = over_core(x1)
    early = beside(0, send)
    z_kept = pack([(z, 0, rows)], [early[0]])
    x1z = over_x(z_kept, True)
    z_o = over_core(z_kept)
    y2 = over_y(x2, True)
    x2_o = over_core(x2)
    low = DIRECT + odd * left
    x2zp = over_x(pack([(z_kept, low, left), (x1z, low, left)], [x2]), False)
    send = pack([(z_kept, 0, DIRECT), (x1z, 0, DIRECT)])
    x2zd = over_x(send, False)
    x1z_o = over_core(x1z)
    y2_o = over_core(y2)
    y2z = over_y(x2zp, True)
    x2zp_o = over_core(x2zp)
    late = beside(1, x2zp)
    x2zd_o = over_core(x2zd)
    y2z_o = over_core(y2z)
    own = [table, x1, x2, y2, z_kept, x1z, x2zp, x2zd, y2z]
    other = [table_o, x1_o, x2_o, y2_o, z_o, x1z_o, x2zp_o, x2zd_o, y2z_o]
    return own + other, early, late


def places(rows, x, core, zhi, odd):
    half, left = rows // 2, (rows - DIRECT) // 2
    found = []
    for q in range(2):
        cc = core ^ q
        d1 = XA + (XB - XA) * cc
        cols = [[256 * ((zhi ^ zz) * 8 + xx * 2 + cc) for xx in (x, x ^ d1, x ^ d1 ^ 2, x ^ 2)] for zz in range(2)]
        for zz, k, piece, source, count, row in (
            (0, 0, 0, 0, rows, 0),
            (0, 1, 1, 0, rows, 0),
            (1, 0, 4, 0, rows, 0),
            (1, 1, 5, 0, rows, 0),
            (0, 2, 2, 0, half, odd * half),
            (0, 3, 2, half, half, odd * half),
            (0, 2, 3, 0, half, (1 - odd) * half),
            (0, 3, 3, half, half, (1 - odd) * half),
            (1, 2, 6, 0, left, DIRECT + odd * left),
            (1, 3, 6, left, left, DIRECT + odd * left),
            (1, 2, 7, 0, DIRECT, 0),
            (1, 3, 7, DIRECT, DIRECT, 0),
            (1, 2, 8, 0, left, DIRECT + (1 - odd) * left),
            (1, 3, 8, left, left, DIRECT + (1 - odd) * left),
        ):
            found.append((zz * 2 + k if k < 2 else 2 + zz * 2 + k, q, 9 * q + piece, source, count, row, cols[zz][k]))
    return sorted(found, key=lambda entry: entry[0])


def main_steps(pieces, position, w, momentum, cots, tokens):
    rows = cots[0].shape[1]
    units, width = w.shape
    many = 8 * units
    scale = 1.0 / math.sqrt(width)
    eps = adam_eps / scale
    first_0 = beta_one * (1.0 - beta_one) / (1.0 - beta_one**2)
    first_1 = (1.0 - beta_one) / (1.0 - beta_one**2)
    second_0 = beta_two * (1.0 - beta_two) / (1.0 - beta_two**2)
    second_1 = (1.0 - beta_two) / (1.0 - beta_two**2)
    keep = 1.0 - inner_rate * decay_rate
    block = 512
    n = len(pieces)
    n_copies = 28

    def kernel(where_ref, *refs):
        piece_refs, (w_hbm, mom_hbm, c0_hbm, c1_hbm), outs = refs[:n], refs[n : n + 4], refs[n + 4 : n + 7]
        table, work, grads, up, cot, ratio, hidden, w_ref, mom_ref, out_ref, sems, more = refs[n + 7 :]
        flat = places(rows, *(where_ref[k] for k in range(4)))

        def start(source, target, sem):
            copy = pltpu.make_async_copy(source, target, sem)
            copy.start()
            return copy

        load_w = start(w_hbm, w_ref, more.at[0])
        copies = []
        for k, (_, _, piece, source, count, row, col) in enumerate(flat):
            row, col = pl.multiple_of(row, 16), pl.multiple_of(col, 256)
            copies.append(
                start(
                    piece_refs[piece].at[pl.ds(source, count), :],
                    table.at[pl.ds(row, count), pl.ds(col, 256)],
                    sems.at[k],
                )
            )
            if k == n_copies // 2:
                load_c = start(c0_hbm, cot, more.at[1])
                load_m = start(mom_hbm, mom_ref, more.at[2])
        load_w.wait()
        for g in range(8):
            for k in range(n_copies):
                if flat[k][0] == g:
                    copies[k].wait()
            for q in range(2):
                col = next(entry[6] for entry in flat if entry[:2] == (g, q))
                cols = pl.ds(pl.multiple_of(col, 256), 256)
                part = lax.dot_general(
                    w_ref[:, cols], table[:, cols], (((1,), (1,)), ((), ())), preferred_element_type=jnp.float32
                )
                if g == 0 and q == 0:
                    hidden[...] = part
                else:
                    hidden[...] += part
        load_c.wait()
        for at in range(0, rows, block):
            cols = slice(at, at + block)
            factor = slope(hidden[:, cols] * scale) * (1.0 / tokens)
            for m in range(8):
                span = slice(m * units, (m + 1) * units)
                up[span, cols] = (cot[span, cols].astype(jnp.float32) * factor).astype(jnp.bfloat16)
        load_c = start(c1_hbm, cot, more.at[1])

        @pl.loop(0, width // block)
        def _(i):
            cols = pl.ds(pl.multiple_of(i * block, block), block)
            grad = jnp.dot(up[...], table[:, cols], preferred_element_type=jnp.float32)
            kept = w_ref[:, cols].astype(jnp.float32) * keep
            total = jnp.zeros(kept.shape, jnp.float32)
            for m in range(8):
                span = slice(m * units, (m + 1) * units)
                g = grad[span]
                r = g * pl.reciprocal(jnp.abs(g) + eps, approx=True)
                total = total + r
                work[span, cols] = (kept - inner_rate * r).astype(jnp.bfloat16)
                grads[span, cols] = g.astype(jnp.bfloat16)
            ratio[:, cols] = total

        load_c.wait()

        @pl.loop(0, rows // block)
        def _(t):
            at = pl.ds(pl.multiple_of(t * block, block), block)
            h = lax.dot_general(
                work[...], table[at, :], (((1,), (1,)), ((), ())), preferred_element_type=jnp.float32
            )
            up[:, at] = (cot[:, at].astype(jnp.float32) * (slope(h * scale) * (1.0 / tokens))).astype(jnp.bfloat16)

        load_m.wait()

        @pl.loop(0, width // block)
        def _(i):
            cols = pl.ds(pl.multiple_of(i * block, block), block)
            grad = jnp.dot(up[...], table[:, cols], preferred_element_type=jnp.float32)
            start_w = w_ref[:, cols].astype(jnp.float32)
            total = jnp.zeros(start_w.shape, jnp.float32)
            for m in range(8):
                span = slice(m * units, (m + 1) * units)
                g1 = grad[span]
                g0 = grads[span, cols].astype(jnp.float32)
                v = (second_0 * g0) * g0 + (second_1 * g1) * g1 + 1e-30
                total = total + (first_0 * g0 + first_1 * g1) * pl.reciprocal(v * lax.rsqrt(v) + eps, approx=True)
            mean = (1.0 - keep * keep) * start_w + (inner_rate / 8.0) * (keep * ratio[:, cols] + total)
            moment = outer_moment * mom_ref[:, cols].astype(jnp.float32) + mean
            out_ref[:, cols] = (start_w - outer_rate * (mean + outer_moment * moment)).astype(jnp.bfloat16)

        for out, (low, size) in zip(outs, PARTS):
            out[...] = out_ref[:, low : low + size]

    return pl.pallas_call(
        kernel,
        in_specs=[pl.BlockSpec(memory_space=pltpu.SMEM)] + [pl.BlockSpec(memory_space=pltpu.HBM)] * (n + 4),
        out_specs=[pl.BlockSpec(memory_space=pltpu.VMEM)] * 3,
        out_shape=[jax.ShapeDtypeStruct((units, size), jnp.bfloat16) for _, size in PARTS],
        scratch_shapes=[
            pltpu.VMEM((rows, width), jnp.bfloat16),
            pltpu.VMEM((many, width), jnp.bfloat16),
            pltpu.VMEM((many, width), jnp.bfloat16),
            pltpu.VMEM((many, rows), jnp.bfloat16),
            pltpu.VMEM((many, rows), jnp.bfloat16),
            pltpu.VMEM((units, width), jnp.float32),
            pltpu.VMEM((units, rows), jnp.float32),
            pltpu.VMEM((units, width), jnp.bfloat16),
            pltpu.VMEM((units, width), jnp.bfloat16),
            pltpu.VMEM((units, width), jnp.bfloat16),
            pltpu.SemaphoreType.DMA((n_copies,)),
            pltpu.SemaphoreType.DMA((3,)),
        ],
        compiler_params=pltpu.CompilerParams(vmem_limit_bytes=60 * MB),
        cost_estimate=pl.CostEstimate(flops=52 * units * rows * width, bytes_accessed=rows * width * 2, transcendentals=0),
        name="main_steps",
    )(position, *pieces, w, momentum, *cots)


def spread(new):
    held = [[(part, 0)] for part in new]
    for step in range(3):
        sends = [part[0][0] if step == 0 else jnp.concatenate([block for block, _ in part]) for part in held]
        sends = lax.optimization_barrier(tuple(sends))
        for part, order, send in zip(held, ORDERS, sends):
            part.append((over_island(send, order[step]), step))
    found = []
    for part, (e1, e2, e3) in zip(held, ORDERS):
        own, r1, r2, r3 = (block for block, _ in part)
        found.append([(own, (0,)), (r1, (e1,)), (r2, (e2, e2 ^ e1)), (r3, (e3, e3 ^ e1, e3 ^ e2, e3 ^ e2 ^ e1))])
    return found


def assemble(found, island, units, width):
    operands, copies = [], [[] for _ in PARTS]
    for p, pieces in enumerate(found):
        for array, froms in pieces:
            for j, mask in enumerate(froms):
                copies[p].append((len(operands), j * units, units, 0, mask))
            operands.append(array)
    total = sum(len(c) for c in copies)
    n = len(operands)
    where = jnp.stack([(island ^ m) * units for m in range(8)]).astype(jnp.int32)

    def kernel(where_ref, *refs):
        arrays, out, held, turned, sems, out_sems = refs[:n], refs[n], refs[n + 1], refs[n + 2], refs[n + 3], refs[n + 4]
        k, waits = 0, []
        for (low, length), group in zip(PARTS, copies):
            mine = []
            for piece, source, size, place, mask in group:
                row = pl.multiple_of(where_ref[mask] + place, 16)
                copy = pltpu.make_async_copy(
                    arrays[piece].at[pl.ds(source, size), :],
                    held.at[pl.ds(row, size), pl.ds(low, length)],
                    sems.at[k],
                )
                copy.start()
                mine.append(copy)
                k += 1
            waits.append(mine)
        outs = []
        for p, ((low, length), mine) in enumerate(zip(PARTS, waits)):
            for copy in mine:
                copy.wait()
            for col in range(low, low + length, 128):
                turned[col : col + 128, :] = held[:, col : col + 128].T
            copy = pltpu.make_async_copy(
                turned.at[pl.ds(low, length), :], out.at[pl.ds(low, length), :], out_sems.at[p]
            )
            copy.start()
            outs.append(copy)
        for copy in outs:
            copy.wait()

    return pl.pallas_call(
        kernel,
        in_specs=[pl.BlockSpec(memory_space=pltpu.SMEM)] + [pl.BlockSpec(memory_space=pltpu.HBM)] * n,
        out_specs=pl.BlockSpec(memory_space=pltpu.HBM),
        out_shape=jax.ShapeDtypeStruct((width, 8 * units), jnp.bfloat16),
        scratch_shapes=[
            pltpu.VMEM((8 * units, width), jnp.bfloat16),
            pltpu.VMEM((width, 8 * units), jnp.bfloat16),
            pltpu.SemaphoreType.DMA((total,)),
            pltpu.SemaphoreType.DMA((len(PARTS),)),
        ],
        compiler_params=pltpu.CompilerParams(vmem_limit_bytes=24 * MB),
        cost_estimate=pl.CostEstimate(flops=0, bytes_accessed=32 * units * width, transcendentals=0),
        name="assemble",
    )(where, *operands)


def body(weights, momentum, table, token_ids, cotangent):
    island, fsdp = lax.axis_index("island"), lax.axis_index("fsdp")
    width, hidden_units = weights.shape
    steps, tokens = token_ids.shape[1:]
    rows = table.shape[0]
    units = hidden_units // 8
    messages = turn_cotangent(cotangent[0], token_ids[0], island)
    arrived = [messages[0]] + [over_island(messages[m], m) for m in range(1, 8)]
    def beside(part, after):
        if part == 0:
            return own_rows(weights, momentum, island, after)
        return [add_by_row(arrived, rows, step, steps, after) for step in range(steps)]

    pieces, (w, mom), cots = gather_pieces(table, messages, island, beside)
    position = jnp.stack([(fsdp // 2) % 4, fsdp % 2, fsdp // 8, island % 2]).astype(jnp.int32)
    new = main_steps(pieces, position, w, mom, cots, tokens)
    return assemble(spread(new), island, units, width)


def solution(mesh):
    placed = (
        P(None, "fsdp"),
        P(None, "fsdp"),
        P(None, "fsdp"),
        P("island", None, None),
        P("island", None, None, "fsdp"),
    )
    return jax.shard_map(body, mesh=mesh, in_specs=placed, out_specs=P(None, "fsdp"), check_vma=False)
```

time: 404 us -> 262 us (0.65)
  waiting for transfers between devices: 282 us -> 96.4 us
  Pallas kernels: 0 us -> 105 us
  matrix products: 84.8 us -> 0 us
  starting transfers between devices: 0.09 us -> 32.2 us
  between operations: 13.2 us -> 0.55 us
  local copies, waits for them, and re-layouts: 8.19 us -> 18.7 us
  other arithmetic: 14 us -> 6.4 us
    psum x1 -> x0, waiting for transfers between devices: 166 us -> none  [body(): total = lax.psum(delta.astype(jnp.bfloat16), 'island').astype(jnp.float32)]
    all_gather x2 -> x0, waiting for transfers between devices: 115 us -> none  [inner_grad(): whole = lax.all_gather(x_local, 'fsdp', axis=1, tiled=True)]
    pallas_call x0 -> x10, Pallas kernels: none -> 105 us  [the longest x1 75.7 us: main_steps(): pl.pallas_call(kernel, in_specs=[pl.BlockSpec(memory_space=pltpu.SMEM)] +...]
    ppermute x0 -> x33, waiting for transfers between devices: none -> 96.4 us  [swap(): return lax.ppermute(a, AXES, pairs)]
    dot_general x3 -> x0, matrix products: 84.8 us -> none  [the longest x2 62.7 us: grad_rows(): lax.dot_general(inputs, upstream, (((0,), (0,)), ((), ())), preferred_ele...]
    ppermute x0 -> x33, starting transfers between devices: none -> 32.2 us  [swap(): return lax.ppermute(a, AXES, pairs)]
    unnamed x6 -> x60, local copies, waits for them, and re-layouts: 0.4 us -> 18.6 us
    convert_element_type x1 -> x0, other arithmetic: 12.1 us -> none  [outer_update(): (base - outer_rate * (mean + outer_moment * moment)).astype(jnp.bfloat16)]
  transfers between devices with their start and end apart: 3 -> 33, of which waited for: 3 -> 14; matrix products, arithmetic and copies ran while one was open for 8% -> 2% of each run, Pallas kernels for 0% -> 9%
where the time goes in v2:
time: 262 us; the launch traced here: 259 us
  Pallas kernels  105 us (40%)
  waiting for transfers between devices  96.4 us (37%)
  starting transfers between devices  32.2 us (12%)
  local copies, waits for them, and re-layouts  18.7 us (7%)
  other arithmetic  6.4 us (2%)
    ppermute x33, waiting for transfers between devices, swap(): return lax.ppermute(a, AXES, pairs)  96.4 us
    pallas_call x1, Pallas kernels, main_steps(): pl.pallas_call(kernel, in_specs=[pl.BlockSpec(memory_space=pltpu.SMEM)] +...  75.7 us
    ppermute x33, starting transfers between devices, swap(): return lax.ppermute(a, AXES, pairs)  32.2 us
    unnamed x60, local copies, waits for them, and re-layouts  18.6 us
    pallas_call x2, Pallas kernels, add_by_row(): pl.pallas_call(kernel, in_specs=[pl.BlockSpec(memory_space=pltpu.VMEM)] *...  10.8 us
    pallas_call x1, Pallas kernels, assemble(): pl.pallas_call(kernel, in_specs=[pl.BlockSpec(memory_space=pltpu.SMEM)] +...  6.21 us
  transfers between devices with their start and end apart: 33, of which 14 were waited for; matrix products, arithmetic and copies ran while one was open for 2% of the time, Pallas kernels for 9%

profile of v2, /device:TPU:70, one launch (start us, length us, event | category | flops | bytes accessed | tf_op | source)
XLA Modules:
  0.0 259.5 jit_solution(104120545903143113)
XLA Ops:
  1.5 4.6 %turn_cotangent.1 = (bf16[240,896]{1,0:T(8,128)(2,1)}, bf16[240,896]{1,0:T(8,128)(2,1)}, bf16[240,896]{1,0:T(8,128)(2,1)}, bf16[240,896]{1,0:T(8,128)(2,1)}, bf1...) custom-call(s32[8]{0:T(128)} %xor_multiply_fusion.where_ref, ...), custom_call_target="tpu_custom_call" | custom-call | bytes 1024 | tf_op jit(solution)/shard_map/turn_cotangent/pallas_call | solution.py:107
  6.1 1.7 collective-permute-start.17
  7.7 2.9 %collective-permute-start.18 = (bf16[240,896]{1,0:T(8,128)(2,1)}, bf16[240,896]{1,0:T(8,128)(2,1)}, u32[]{:S(2)}, u32[]{:S(2)}) collective-permute-start(bf16[240,896]{1,0:T(8,128)(2,1)} %get-tuple-element.31), channel_id=1, source_target_pairs={{0,32},{1,33},{2,34},{3,35},{4,36},{5,37},{6,38},{7,39},{8,40},{9,... | collective-permute-start | bytes 1290248 | tf_op jit(solution)/shard_map/ppermute | solution.py:42
  10.9 4.1 %collective-permute-done.refs_1_ = bf16[2048,256]{1,0:T(8,128)(2,1)S(1)} collective-permute-done((bf16[2048,256]{1,0:T(8,128)(2,1)}, bf16[2048,256]{1,0:T(8,128)(2,1)S(1)}, u32[]{:S(2)}, u32[]{:S(2)}) %collective-permute-start) | collective-permute-done | bytes 1048608 | tf_op jit(solution)/shard_map/ppermute | solution.py:42
  15.0 1.6 collective-permute-start.20
  18.2 1.6 pack.4._
  20.8 4.6 %own_rows.1 = (bf16[112,4096]{1,0:T(8,128)(2,1)}, bf16[112,4096]{1,0:T(8,128)(2,1)}) custom-call(s32[2]{0:T(128)} %pad_add_fusion.2.where_ref, bf16[4096,896]{1,0:T(8,128)(2,1)} %w_ref.1, bf16[4096,896]{1,0:T(8,128)(2,1)} %m_ref.1, bf16[2048,256]{1,0:T(8,128)(2,1)} %copy-done.1), custom_call_target="tpu_custom_call" | custom-call | bytes 1024 | tf_op jit(solution)/shard_map/own_rows/pallas_call | solution.py:150
  30.5 2.6 %collective-permute-start.1 = (bf16[2048,256]{1,0:T(8,128)(2,1)S(1)}, bf16[2048,256]{1,0:T(8,128)(2,1)}, u32[]{:S(2)}, u32[]{:S(2)}) collective-permute-start(bf16[2048,256]{1,0:T(8,128)(2,1)S(1)} %copy-done.2), channel_id=1, source_target_pairs={{0,6},{1,3},{2,4},{3,1},{4,2},{5,7},{6,0},{7,5},{8,14},{9,11},{10,... | collective-permute-start | bytes 3145736 | tf_op jit(solution)/shard_map/ppermute | solution.py:42
  33.1 3.8 %collective-permute-start.21 = (bf16[240,896]{1,0:T(8,128)(2,1)S(1)}, bf16[240,896]{1,0:T(8,128)(2,1)S(1)}, u32[]{:S(2)}, u32[]{:S(2)}) collective-permute-start(bf16[240,896]{1,0:T(8,128)(2,1)S(1)} %copy-done.29), channel_id=1, source_target_pairs={{0,80},{1,81},{2,82},{3,83},{4,84},{5,85},{6,86},{7,87},{8,88},{9,... | collective-permute-start | bytes 1290248 | tf_op jit(solution)/shard_map/ppermute | solution.py:42
  37.0 1.7 collective-permute-start.22
  39.4 8.3 %collective-permute-done.21.refs_5_ = bf16[240,896]{1,0:T(8,128)(2,1)S(1)} collective-permute-done((bf16[240,896]{1,0:T(8,128)(2,1)S(1)}, bf16[240,896]{1,0:T(8,128)(2,1)S(1)}, u32[]{:S(2)}, u32[]{:S(2)}) %collective-permute-start.21) | collective-permute-done | bytes 430112 | tf_op jit(solution)/shard_map/ppermute | solution.py:42
  48.6 7.7 %collective-permute-done.22.refs_6_ = bf16[240,896]{1,0:T(8,128)(2,1)S(1)} collective-permute-done((bf16[240,896]{1,0:T(8,128)(2,1)S(1)}, bf16[240,896]{1,0:T(8,128)(2,1)S(1)}, u32[]{:S(2)}, u32[]{:S(2)}) %collective-permute-start.22) | collective-permute-done | bytes 430112 | tf_op jit(solution)/shard_map/ppermute | solution.py:42
  57.0 2.6 collective-permute-start.23
  60.5 11.7 %collective-permute-done.23.refs_7_ = bf16[240,896]{1,0:T(8,128)(2,1)} collective-permute-done((bf16[240,896]{1,0:T(8,128)(2,1)}, bf16[240,896]{1,0:T(8,128)(2,1)}, u32[]{:S(2)}, u32[]{:S(2)}) %collective-permute-start.23) | collective-permute-done | bytes 430112 | tf_op jit(solution)/shard_map/ppermute | solution.py:42
  72.3 1.7 collective-permute-start.5
  74.9 1.6 collective-permute-start.6
  76.6 7.5 %collective-permute-done.5.refs_8_.refs_6_ = bf16[1280,256]{1,0:T(8,128)(2,1)S(1)} collective-permute-done((bf16[1280,256]{1,0:T(8,128)(2,1)S(1)}, bf16[1280,256]{1,0:T(8,128)(2,1)S(1)}, u32[]{:S(2)}, u32[]{:S(2)}) %collective-permute-start.5) | collective-permute-done | bytes 655392 | tf_op jit(solution)/shard_map/ppermute | solution.py:42
  84.7 7.9 %collective-permute-done.6.refs_7_ = bf16[1536,256]{1,0:T(8,128)(2,1)} collective-permute-done((bf16[1536,256]{1,0:T(8,128)(2,1)S(1)}, bf16[1536,256]{1,0:T(8,128)(2,1)}, u32[]{:S(2)}, u32[]{:S(2)}) %collective-permute-start.6) | collective-permute-done | bytes 786464 | tf_op jit(solution)/shard_map/ppermute | solution.py:42
  98.8 5.4 %add_by_row.3.refs_21_ = bf16[896,2048]{1,0:T(8,128)(2,1)S(1)} custom-call(bf16[240,896]{1,0:T(8,128)(2,1)S(1)} %copy-done.15, bf16[240,896]{1,0:T(8,128)(2,1)} %collective-permute-done.17.refs_1_, bf16[240,896]{1,0:T(8,128)(2,1)} %collective-permute-done.18.refs_2_, bf16[240,896]{1,0:T(8,128)(2,1)} %collective-permute-done.19.refs_3_, ...), custom_call_target="tpu_custom_call" | custom-call | flops 4000000000 | bytes 7340032 | tf_op jit(solution)/shard_map/add_by_row/pallas_call | solution.py:186
  104.2 1.8 copy-done.22
  106.0 5.4 %add_by_row.2.refs_20_ = bf16[896,2048]{1,0:T(8,128)(2,1)S(1)} custom-call(bf16[240,896]{1,0:T(8,128)(2,1)S(1)} %copy-done.15, bf16[240,896]{1,0:T(8,128)(2,1)} %collective-permute-done.17.refs_1_, bf16[240,896]{1,0:T(8,128)(2,1)} %collective-permute-done.18.refs_2_, bf16[240,896]{1,0:T(8,128)(2,1)} %collective-permute-done.19.refs_3_, ...), custom_call_target="tpu_custom_call" | custom-call | flops 4000000000 | bytes 7340032 | tf_op jit(solution)/shard_map/add_by_row/pallas_call | solution.py:186
  111.4 1.8 copy-done.23
  114.9 75.7 %main_steps.1 = (bf16[112,1408]{1,0:T(8,128)(2,1)}, bf16[112,1408]{1,0:T(8,128)(2,1)}, bf16[112,1280]{1,0:T(8,128)(2,1)}) custom-call(s32[4]{0:T(128)} %pad_add_fusion.where_ref, bf16[2048,256]{1,0:T(8,128)(2,1)} %refs_0_.3, bf16[2048,256]{1,0:T(8,128)(2,1)} %copy-done.9, bf16[2048,256]{1,0:T(8,128)(2,1)} %collective-permute-done.1.refs_2_, ...), custom_call_target="tpu_custom_call" | custom-call | flops 48855252992 | bytes 16777216 | tf_op jit(solution)/shard_map/main_steps/pallas_call | solution.py:395
  190.6 2.6 %collective-permute-start.26 = (bf16[112,1280]{1,0:T(8,128)(2,1)}, bf16[112,1280]{1,0:T(8,128)(2,1)S(1)}, u32[]{:S(2)}, u32[]{:S(2)}) collective-permute-start(bf16[112,1280]{1,0:T(8,128)(2,1)} %get-tuple-element.42), channel_id=1, source_target_pairs={{0,64},{1,65},{2,66},{3,67},{4,68},{5,69},{6,70},{7,71},{8,72},{9,... | collective-permute-start | bytes 860168 | tf_op jit(solution)/shard_map/ppermute | solution.py:42
  193.6 7.3 %collective-permute-done.26.refs_9_ = bf16[112,1280]{1,0:T(8,128)(2,1)S(1)} collective-permute-done((bf16[112,1280]{1,0:T(8,128)(2,1)}, bf16[112,1280]{1,0:T(8,128)(2,1)S(1)}, u32[]{:S(2)}, u32[]{:S(2)}) %collective-permute-start.26) | collective-permute-done | bytes 286752 | tf_op jit(solution)/shard_map/ppermute | solution.py:42
  202.0 2.3 collective-permute-done.25.refs_5_
  204.9 1.9 collective-permute-start.27
  206.8 12.0 %collective-permute-done.29.refs_10_ = bf16[224,1280]{1,0:T(8,128)(2,1)S(1)} collective-permute-done((bf16[224,1280]{1,0:T(8,128)(2,1)S(1)}, bf16[224,1280]{1,0:T(8,128)(2,1)S(1)}, u32[]{:S(2)}, u32[]{:S(2)}) %collective-permute-start.29) | collective-permute-done | bytes 573472 | tf_op jit(solution)/shard_map/ppermute | solution.py:42
  222.8 1.3 collective-permute-start.30
  224.7 1.4 collective-permute-start.32
  226.2 25.2 %collective-permute-done.32.refs_11_ = bf16[448,1280]{1,0:T(8,128)(2,1)} collective-permute-done((bf16[448,1280]{1,0:T(8,128)(2,1)}, bf16[448,1280]{1,0:T(8,128)(2,1)}, u32[]{:S(2)}, u32[]{:S(2)}) %collective-permute-start.32) | collective-permute-done | bytes 1146912 | tf_op jit(solution)/shard_map/ppermute | solution.py:42
  253.1 6.2 %assemble.1 = bf16[4096,896]{1,0:T(8,128)(2,1)} custom-call(s32[8]{0:T(128)S(1)} %stack.73.where_ref, bf16[112,1408]{1,0:T(8,128)(2,1)S(1)} %copy-done.4, bf16[112,1408]{1,0:T(8,128)(2,1)S(1)} %collective-permute-done.24.refs_1_, bf16[224,1408]{1,0:T(8,128)(2,1)S(1)} %collective-permute-done.27.refs_2_, bf16[448,1408]{1,0:T(8,128)(2,1)} %collective-permute-done.30.refs_3_, ...), custom_call_target="tpu_custom_call" | custom-call | bytes 14680064 | tf_op jit(solution)/shard_map/assemble/pallas_call | solution.py:475
  (117 shorter events, 30.4 us)
Async XLA Ops:
  0.0 15.0 %collective-permute-start = (bf16[2048,256]{1,0:T(8,128)(2,1)}, bf16[2048,256]{1,0:T(8,128)(2,1)S(1)}, u32[]{:S(2)}, u32[]{:S(2)}) collective-permute-start(bf16[2048,256]{1,0:T(8,128)(2,1)} %refs_0_.3), channel_id=1, source_target_pairs={{0,2},{1,7},{2,0},{3,5},{4,6},{5,3},{6,4},{7,1},{8,10},{9,15},{10,... | collective-permute-start | bytes 3145736 | tf_op jit(solution)/shard_map/ppermute | solution.py:42
  0.8 24.6 %collective-permute-start.3 = (bf16[2048,256]{1,0:T(8,128)(2,1)}, bf16[2048,256]{1,0:T(8,128)(2,1)S(1)}, u32[]{:S(2)}, u32[]{:S(2)}) collective-permute-start(bf16[2048,256]{1,0:T(8,128)(2,1)} %refs_0_.3), channel_id=1, source_target_pairs={{0,72},{1,73},{2,74},{3,75},{4,76},{5,77},{6,78},{7,79},{8,64},{9,... | collective-permute-start | bytes 3145736 | tf_op jit(solution)/shard_map/ppermute | solution.py:42
  6.1 23.8 %collective-permute-start.17 = (bf16[240,896]{1,0:T(8,128)(2,1)}, bf16[240,896]{1,0:T(8,128)(2,1)}, u32[]{:S(2)}, u32[]{:S(2)}) collective-permute-start(bf16[240,896]{1,0:T(8,128)(2,1)} %get-tuple-element.27.refs_2_), channel_id=1, source_target_pairs={{0,16},{1,17},{2,18},{3,19},{4,20},{5,21},{6,22},{7,23},{8,24},{9,... | collective-permute-start | bytes 1290248 | tf_op jit(solution)/shard_map/ppermute | solution.py:42
  7.7 25.4 %collective-permute-start.18 = (bf16[240,896]{1,0:T(8,128)(2,1)}, bf16[240,896]{1,0:T(8,128)(2,1)}, u32[]{:S(2)}, u32[]{:S(2)}) collective-permute-start(bf16[240,896]{1,0:T(8,128)(2,1)} %get-tuple-element.31), channel_id=1, source_target_pairs={{0,32},{1,33},{2,34},{3,35},{4,36},{5,37},{6,38},{7,39},{8,40},{9,... | collective-permute-start | bytes 1290248 | tf_op jit(solution)/shard_map/ppermute | solution.py:42
  10.6 26.3 %collective-permute-start.19 = (bf16[240,896]{1,0:T(8,128)(2,1)}, bf16[240,896]{1,0:T(8,128)(2,1)}, u32[]{:S(2)}, u32[]{:S(2)}) collective-permute-start(bf16[240,896]{1,0:T(8,128)(2,1)} %get-tuple-element.32), channel_id=1, source_target_pairs={{0,48},{1,49},{2,50},{3,51},{4,52},{5,53},{6,54},{7,55},{8,56},{9,... | collective-permute-start | bytes 1290248 | tf_op jit(solution)/shard_map/ppermute | solution.py:42
  15.0 23.7 %collective-permute-start.20 = (bf16[240,896]{1,0:T(8,128)(2,1)}, bf16[240,896]{1,0:T(8,128)(2,1)S(1)}, u32[]{:S(2)}, u32[]{:S(2)}) collective-permute-start(bf16[240,896]{1,0:T(8,128)(2,1)} %get-tuple-element.33), channel_id=1, source_target_pairs={{0,64},{1,65},{2,66},{3,67},{4,68},{5,69},{6,70},{7,71},{8,72},{9,... | collective-permute-start | bytes 1290248 | tf_op jit(solution)/shard_map/ppermute | solution.py:42
  29.0 30.6 %collective-permute-start.4 = (bf16[2048,256]{1,0:T(8,128)(2,1)S(1)}, bf16[2048,256]{1,0:T(8,128)(2,1)S(1)}, u32[]{:S(2)}, u32[]{:S(2)}) collective-permute-start(bf16[2048,256]{1,0:T(8,128)(2,1)S(1)} %pack.5.refs_0_.refs_4_), channel_id=1, source_target_pairs={{0,2},{1,7},{2,0},{3,5},{4,6},{5,3},{6,4},{7,1},{8,10},{9,15},{10,... | collective-permute-start | bytes 3145736 | tf_op jit(solution)/shard_map/ppermute | solution.py:42
  30.5 29.1 %collective-permute-start.1 = (bf16[2048,256]{1,0:T(8,128)(2,1)S(1)}, bf16[2048,256]{1,0:T(8,128)(2,1)}, u32[]{:S(2)}, u32[]{:S(2)}) collective-permute-start(bf16[2048,256]{1,0:T(8,128)(2,1)S(1)} %copy-done.2), channel_id=1, source_target_pairs={{0,6},{1,3},{2,4},{3,1},{4,2},{5,7},{6,0},{7,5},{8,14},{9,11},{10,... | collective-permute-start | bytes 3145736 | tf_op jit(solution)/shard_map/ppermute | solution.py:42
  33.1 14.7 %collective-permute-start.21 = (bf16[240,896]{1,0:T(8,128)(2,1)S(1)}, bf16[240,896]{1,0:T(8,128)(2,1)S(1)}, u32[]{:S(2)}, u32[]{:S(2)}) collective-permute-start(bf16[240,896]{1,0:T(8,128)(2,1)S(1)} %copy-done.29), channel_id=1, source_target_pairs={{0,80},{1,81},{2,82},{3,83},{4,84},{5,85},{6,86},{7,87},{8,88},{9,... | collective-permute-start | bytes 1290248 | tf_op jit(solution)/shard_map/ppermute | solution.py:42
  37.0 19.3 %collective-permute-start.22 = (bf16[240,896]{1,0:T(8,128)(2,1)S(1)}, bf16[240,896]{1,0:T(8,128)(2,1)S(1)}, u32[]{:S(2)}, u32[]{:S(2)}) collective-permute-start(bf16[240,896]{1,0:T(8,128)(2,1)S(1)} %copy-done.28), channel_id=1, source_target_pairs={{0,96},{1,97},{2,98},{3,99},{4,100},{5,101},{6,102},{7,103},{8,104... | collective-permute-start | bytes 1290248 | tf_op jit(solution)/shard_map/ppermute | solution.py:42
  39.4 34.5 %collective-permute-start.8 = (bf16[2048,256]{1,0:T(8,128)(2,1)}, bf16[2048,256]{1,0:T(8,128)(2,1)}, u32[]{:S(2)}, u32[]{:S(2)}) collective-permute-start(bf16[2048,256]{1,0:T(8,128)(2,1)} %refs_0_.3), channel_id=1, source_target_pairs={{0,1},{1,0},{2,3},{3,2},{4,5},{5,4},{6,7},{7,6},{8,9},{9,8},{10,11... | collective-permute-start | bytes 3145736 | tf_op jit(solution)/shard_map/ppermute | solution.py:42
  48.6 26.4 %collective-permute-start.12 = (bf16[2048,256]{1,0:T(8,128)(2,1)S(1)}, bf16[2048,256]{1,0:T(8,128)(2,1)}, u32[]{:S(2)}, u32[]{:S(2)}) collective-permute-start(bf16[2048,256]{1,0:T(8,128)(2,1)S(1)} %pack.5.refs_0_.refs_4_), channel_id=1, source_target_pairs={{0,1},{1,0},{2,3},{3,2},{4,5},{5,4},{6,7},{7,6},{8,9},{9,8},{10,11... | collective-permute-start | bytes 3145736 | tf_op jit(solution)/shard_map/ppermute | solution.py:42
  57.0 15.3 %collective-permute-start.23 = (bf16[240,896]{1,0:T(8,128)(2,1)}, bf16[240,896]{1,0:T(8,128)(2,1)}, u32[]{:S(2)}, u32[]{:S(2)}) collective-permute-start(bf16[240,896]{1,0:T(8,128)(2,1)} %get-tuple-element.36), channel_id=1, source_target_pairs={{0,112},{1,113},{2,114},{3,115},{4,116},{5,117},{6,118},{7,119},{8... | collective-permute-start | bytes 1290248 | tf_op jit(solution)/shard_map/ppermute | solution.py:42
  59.6 24.5 %collective-permute-start.9 = (bf16[2048,256]{1,0:T(8,128)(2,1)}, bf16[2048,256]{1,0:T(8,128)(2,1)}, u32[]{:S(2)}, u32[]{:S(2)}) collective-permute-start(bf16[2048,256]{1,0:T(8,128)(2,1)} %copy-done.9), channel_id=1, source_target_pairs={{0,1},{1,0},{2,3},{3,2},{4,5},{5,4},{6,7},{7,6},{8,9},{9,8},{10,11... | collective-permute-start | bytes 3145736 | tf_op jit(solution)/shard_map/ppermute | solution.py:42
  59.6 24.6 %collective-permute-start.2 = (bf16[2048,256]{1,0:T(8,128)(2,1)}, bf16[2048,256]{1,0:T(8,128)(2,1)}, u32[]{:S(2)}, u32[]{:S(2)}) collective-permute-start(bf16[2048,256]{1,0:T(8,128)(2,1)} %collective-permute-done.1.refs_2_), channel_id=1, source_target_pairs={{0,16},{1,49},{2,18},{3,51},{4,20},{5,53},{6,22},{7,55},{8,24},{9,... | collective-permute-start | bytes 3145736 | tf_op jit(solution)/shard_map/ppermute | solution.py:42
  72.3 11.8 %collective-permute-start.5 = (bf16[1280,256]{1,0:T(8,128)(2,1)S(1)}, bf16[1280,256]{1,0:T(8,128)(2,1)S(1)}, u32[]{:S(2)}, u32[]{:S(2)}) collective-permute-start(bf16[1280,256]{1,0:T(8,128)(2,1)S(1)} %pack.6), channel_id=1, source_target_pairs={{0,6},{1,3},{2,4},{3,1},{4,2},{5,7},{6,0},{7,5},{8,14},{9,11},{10,... | collective-permute-start | bytes 1966088 | tf_op jit(solution)/shard_map/ppermute | solution.py:42
  73.9 19.3 %collective-permute-start.13 = (bf16[2048,256]{1,0:T(8,128)(2,1)S(1)}, bf16[2048,256]{1,0:T(8,128)(2,1)}, u32[]{:S(2)}, u32[]{:S(2)}) collective-permute-start(bf16[2048,256]{1,0:T(8,128)(2,1)S(1)} %collective-permute-done.4.refs_1_.refs_5_), channel_id=1, source_target_pairs={{0,1},{1,0},{2,3},{3,2},{4,5},{5,4},{6,7},{7,6},{8,9},{9,8},{10,11... | collective-permute-start | bytes 3145736 | tf_op jit(solution)/shard_map/ppermute | solution.py:42
  74.9 17.7 %collective-permute-start.6 = (bf16[1536,256]{1,0:T(8,128)(2,1)S(1)}, bf16[1536,256]{1,0:T(8,128)(2,1)}, u32[]{:S(2)}, u32[]{:S(2)}) collective-permute-start(bf16[1536,256]{1,0:T(8,128)(2,1)S(1)} %pack.7), channel_id=1, source_target_pairs={{0,6},{1,3},{2,4},{3,1},{4,2},{5,7},{6,0},{7,5},{8,14},{9,11},{10,... | collective-permute-start | bytes 2359304 | tf_op jit(solution)/shard_map/ppermute | solution.py:42
  84.1 10.7 %collective-permute-start.7 = (bf16[1280,256]{1,0:T(8,128)(2,1)S(1)}, bf16[1280,256]{1,0:T(8,128)(2,1)}, u32[]{:S(2)}, u32[]{:S(2)}) collective-permute-start(bf16[1280,256]{1,0:T(8,128)(2,1)S(1)} %collective-permute-done.5.refs_8_.refs_6_), channel_id=1, source_target_pairs={{0,16},{1,49},{2,18},{3,51},{4,20},{5,53},{6,22},{7,55},{8,24},{9,... | collective-permute-start | bytes 1966088 | tf_op jit(solution)/shard_map/ppermute | solution.py:42
  84.1 29.2 %collective-permute-start.10 = (bf16[2048,256]{1,0:T(8,128)(2,1)}, bf16[2048,256]{1,0:T(8,128)(2,1)S(1)}, u32[]{:S(2)}, u32[]{:S(2)}) collective-permute-start(bf16[2048,256]{1,0:T(8,128)(2,1)} %collective-permute-done.1.refs_2_), channel_id=1, source_target_pairs={{0,1},{1,0},{2,3},{3,2},{4,5},{5,4},{6,7},{7,6},{8,9},{9,8},{10,11... | collective-permute-start | bytes 3145736 | tf_op jit(solution)/shard_map/ppermute | solution.py:42
  84.2 29.1 %collective-permute-start.11 = (bf16[2048,256]{1,0:T(8,128)(2,1)}, bf16[2048,256]{1,0:T(8,128)(2,1)}, u32[]{:S(2)}, u32[]{:S(2)}) collective-permute-start(bf16[2048,256]{1,0:T(8,128)(2,1)} %collective-permute-done.2.refs_3_), channel_id=1, source_target_pairs={{0,1},{1,0},{2,3},{3,2},{4,5},{5,4},{6,7},{7,6},{8,9},{9,8},{10,11... | collective-permute-start | bytes 3145736 | tf_op jit(solution)/shard_map/ppermute | solution.py:42
  92.6 20.7 %collective-permute-start.15 = (bf16[1536,256]{1,0:T(8,128)(2,1)}, bf16[1536,256]{1,0:T(8,128)(2,1)S(1)}, u32[]{:S(2)}, u32[]{:S(2)}) collective-permute-start(bf16[1536,256]{1,0:T(8,128)(2,1)} %collective-permute-done.6.refs_7_), channel_id=1, source_target_pairs={{0,1},{1,0},{2,3},{3,2},{4,5},{5,4},{6,7},{7,6},{8,9},{9,8},{10,11... | collective-permute-start | bytes 2359304 | tf_op jit(solution)/shard_map/ppermute | solution.py:42
  93.2 20.0 %collective-permute-start.14 = (bf16[1280,256]{1,0:T(8,128)(2,1)S(1)}, bf16[1280,256]{1,0:T(8,128)(2,1)S(1)}, u32[]{:S(2)}, u32[]{:S(2)}) collective-permute-start(bf16[1280,256]{1,0:T(8,128)(2,1)S(1)} %collective-permute-done.5.refs_8_.refs_6_), channel_id=1, source_target_pairs={{0,1},{1,0},{2,3},{3,2},{4,5},{5,4},{6,7},{7,6},{8,9},{9,8},{10,11... | collective-permute-start | bytes 1966088 | tf_op jit(solution)/shard_map/ppermute | solution.py:42
  94.7 18.5 %collective-permute-start.16 = (bf16[1280,256]{1,0:T(8,128)(2,1)}, bf16[1280,256]{1,0:T(8,128)(2,1)S(1)}, u32[]{:S(2)}, u32[]{:S(2)}) collective-permute-start(bf16[1280,256]{1,0:T(8,128)(2,1)} %collective-permute-done.7.refs_8_), channel_id=1, source_target_pairs={{0,1},{1,0},{2,3},{3,2},{4,5},{5,4},{6,7},{7,6},{8,9},{9,8},{10,11... | collective-permute-start | bytes 1966088 | tf_op jit(solution)/shard_map/ppermute | solution.py:42
  193.3 11.0 %collective-permute-start.25 = (bf16[112,1408]{1,0:T(8,128)(2,1)}, bf16[112,1408]{1,0:T(8,128)(2,1)S(1)}, u32[]{:S(2)}, u32[]{:S(2)}) collective-permute-start(bf16[112,1408]{1,0:T(8,128)(2,1)} %get-tuple-element.39.refs_4_), channel_id=1, source_target_pairs={{0,48},{1,49},{2,50},{3,51},{4,52},{5,53},{6,54},{7,55},{8,56},{9,... | collective-permute-start | bytes 946184 | tf_op jit(solution)/shard_map/ppermute | solution.py:42
  193.6 10.7 %collective-permute-start.24 = (bf16[112,1408]{1,0:T(8,128)(2,1)}, bf16[112,1408]{1,0:T(8,128)(2,1)S(1)}, u32[]{:S(2)}, u32[]{:S(2)}) collective-permute-start(bf16[112,1408]{1,0:T(8,128)(2,1)} %get-tuple-element.37.refs_0_), channel_id=1, source_target_pairs={{0,16},{1,17},{2,18},{3,19},{4,20},{5,21},{6,22},{7,23},{8,24},{9,... | collective-permute-start | bytes 946184 | tf_op jit(solution)/shard_map/ppermute | solution.py:42
  204.4 14.4 %collective-permute-start.29 = (bf16[224,1280]{1,0:T(8,128)(2,1)S(1)}, bf16[224,1280]{1,0:T(8,128)(2,1)S(1)}, u32[]{:S(2)}, u32[]{:S(2)}) collective-permute-start(bf16[224,1280]{1,0:T(8,128)(2,1)S(1)} %pad_maximum_fusion.5), channel_id=1, source_target_pairs={{0,16},{1,17},{2,18},{3,19},{4,20},{5,21},{6,22},{7,23},{8,24},{9,... | collective-permute-start | bytes 1720328 | tf_op jit(solution)/shard_map/ppermute | solution.py:42
  204.5 15.6 %collective-permute-start.28 = (bf16[224,1408]{1,0:T(8,128)(2,1)S(1)}, bf16[224,1408]{1,0:T(8,128)(2,1)S(1)}, u32[]{:S(2)}, u32[]{:S(2)}) collective-permute-start(bf16[224,1408]{1,0:T(8,128)(2,1)S(1)} %pad_maximum_fusion.4), channel_id=1, source_target_pairs={{0,64},{1,65},{2,66},{3,67},{4,68},{5,69},{6,70},{7,71},{8,72},{9,... | collective-permute-start | bytes 1892360 | tf_op jit(solution)/shard_map/ppermute | solution.py:42
  204.9 16.8 %collective-permute-start.27 = (bf16[224,1408]{1,0:T(8,128)(2,1)S(1)}, bf16[224,1408]{1,0:T(8,128)(2,1)S(1)}, u32[]{:S(2)}, u32[]{:S(2)}) collective-permute-start(bf16[224,1408]{1,0:T(8,128)(2,1)S(1)} %pad_maximum_fusion.3), channel_id=1, source_target_pairs={{0,48},{1,49},{2,50},{3,51},{4,52},{5,53},{6,54},{7,55},{8,56},{9,... | collective-permute-start | bytes 1892360 | tf_op jit(solution)/shard_map/ppermute | solution.py:42
  222.8 28.6 %collective-permute-start.30 = (bf16[448,1408]{1,0:T(8,128)(2,1)}, bf16[448,1408]{1,0:T(8,128)(2,1)}, u32[]{:S(2)}, u32[]{:S(2)}) collective-permute-start(bf16[448,1408]{1,0:T(8,128)(2,1)} %pad_maximum_fusion), channel_id=1, source_target_pairs={{0,64},{1,65},{2,66},{3,67},{4,68},{5,69},{6,70},{7,71},{8,72},{9,... | collective-permute-start | bytes 3784712 | tf_op jit(solution)/shard_map/ppermute | solution.py:42
  224.2 27.9 %collective-permute-start.31 = (bf16[448,1408]{1,0:T(8,128)(2,1)}, bf16[448,1408]{1,0:T(8,128)(2,1)}, u32[]{:S(2)}, u32[]{:S(2)}) collective-permute-start(bf16[448,1408]{1,0:T(8,128)(2,1)} %pad_maximum_fusion.1), channel_id=1, source_target_pairs={{0,16},{1,17},{2,18},{3,19},{4,20},{5,21},{6,22},{7,23},{8,24},{9,... | collective-permute-start | bytes 3784712 | tf_op jit(solution)/shard_map/ppermute | solution.py:42
  224.7 26.7 %collective-permute-start.32 = (bf16[448,1280]{1,0:T(8,128)(2,1)}, bf16[448,1280]{1,0:T(8,128)(2,1)}, u32[]{:S(2)}, u32[]{:S(2)}) collective-permute-start(bf16[448,1280]{1,0:T(8,128)(2,1)} %pad_maximum_fusion.2), channel_id=1, source_target_pairs={{0,48},{1,49},{2,50},{3,51},{4,52},{5,53},{6,54},{7,55},{8,56},{9,... | collective-permute-start | bytes 3440648 | tf_op jit(solution)/shard_map/ppermute | solution.py:42
  (31 other events, 174.7 us)
